TPU v7x, 32 devices: a whole 2x2x4 slice. The times are simulated.
32 devices in a mesh: groups: 2 (over y), seq: 4 (over z), head: 2 (over x), sub: 2 (over core).
Axes of the slice: x: 2, y: 2, z: 4, core: 2. Of those that a mesh axis runs over, the one named last changes fastest.
Arguments:
- frames_in: bfloat16 [2048, 1536], P(('groups', 'seq', 'head', 'sub')), parts along dimension 0, may hold values from -30 to 30
- attn_gain: float32 [1536], replicated, may hold values from 0.25 to 1.75
- w_qkv: bfloat16 [1536, 24, 192], P(None, ('head', 'sub')), may hold values from -1 to 1
- w_out: bfloat16 [1536, 1536], P(('head', 'sub')), may hold values from -0.3125 to 0.3125
- vit_gain: float32 [1536], replicated, may hold values from 0.25 to 1.75
- w_pair: bfloat16 [2, 1536, 1024], P(None, None, ('head', 'sub')), may hold values from -0.109375 to 0.109375
- w_act: float32 [1024, 7], P(('head', 'sub')), may hold values from -0.375 to 0.375
- pair_frames: int32 [4, 15], P('groups'), parts along dimension 0, may hold values from 0 to 14, each once within a row
Outputs:
- hidden: bfloat16 [2048, 1536], P(('groups', 'seq', 'head', 'sub')), parts along dimension 0
- actions: float32 [4, 15, 7], P('groups'), parts along dimension 0
There are 2 independent parts, one for each index of `groups`. A program takes and returns all parts, laid end to end along the dimension named above; an argument that names none is the same for every part. Nothing has to cross between parts.
All inputs are finite; a program needn't handle non-finite values.
Results may differ from a plain program's by a relative error of at most 0.01.
Values may be sent and summed in bfloat16 or wider, within the bound.
A program may use at most 64 MiB of HBM per device.

v0:
```python
import jax
import jax.numpy as jnp
from jax import lax
from jax.sharding import PartitionSpec as P

F = 16
ROLLS = 2


def from_behind(value, axis, steps):
    count = lax.axis_size(axis)
    leading, last = (max(0, -steps), min(count, count - steps))
    return lax.ppermute(value, axis, [(source, source + steps) for source in range(leading, last)])


def normalize(values_in, gain_vec):
    floats = values_in.astype(jnp.float32)
    mean_sq = jnp.mean(floats * floats, axis=-1, keepdims=True)
    return (floats * lax.rsqrt(mean_sq + 1e-06) * gain_vec).astype(jnp.bfloat16)


def shards(frames_in, attn_gain, w_qkv, w_out, vit_gain, w_pair, w_act, pair_frames):
    rows_own = frames_in.shape[0]
    model_width = frames_in.shape[1]
    seq_count = lax.axis_size("seq")
    split_count = lax.axis_size(("head", "sub"))
    block_rows = rows_own * split_count
    total_cols = block_rows * seq_count // F
    frames_local = max(1, F // seq_count)
    cols_local = block_rows // frames_local
    frame_step = max(1, seq_count // F)
    heads_local = w_qkv.shape[1]
    triple_dim = w_qkv.shape[2]
    head_dim = triple_dim // 3
    qkv_matrix = w_qkv.reshape(model_width, heads_local * triple_dim)
    normed = lax.all_gather(normalize(frames_in, attn_gain), ("head", "sub"), axis=0, tiled=True)
    qkv_rows = jnp.dot(normed, qkv_matrix, preferred_element_type=jnp.float32).astype(jnp.bfloat16)
    qkv_rows = qkv_rows.reshape(
        frames_local, seq_count, cols_local // seq_count, heads_local, triple_dim
    )
    columns = lax.all_to_all(qkv_rows, "seq", split_axis=1, concat_axis=0, tiled=True)
    item_count = columns.shape[2]
    by_frame = columns.reshape(F, -1, heads_local, triple_dim)
    queries = by_frame[..., :head_dim]
    key_part = by_frame[..., head_dim : 2 * head_dim]
    value_part = by_frame[..., 2 * head_dim :]
    scores = jnp.einsum(
        "fchd,gchd->chfg", queries, key_part, preferred_element_type=jnp.float32
    ) * head_dim ** (-0.5)
    row_peak = jnp.max(scores, axis=-1, keepdims=True)
    weights = jnp.exp(scores - row_peak)
    weights = (weights / jnp.sum(weights, axis=-1, keepdims=True)).astype(jnp.bfloat16)
    mixed_out = jnp.einsum(
        "chfg,gchd->fchd", weights, value_part, preferred_element_type=jnp.float32
    ).astype(jnp.bfloat16)
    mixed_out = mixed_out.reshape(seq_count * frames_local, 1, item_count, heads_local * head_dim)
    attended = lax.all_to_all(mixed_out, "seq", split_axis=0, concat_axis=1, tiled=True)
    attended = attended.reshape(block_rows, heads_local * head_dim)
    branch_sum = lax.psum_scatter(
        jnp.dot(attended, w_out, preferred_element_type=jnp.float32).astype(jnp.bfloat16),
        ("head", "sub"),
        scatter_dimension=0,
        tiled=True,
    ).astype(jnp.float32)
    hidden = (frames_in.astype(jnp.float32) + branch_sum).astype(jnp.bfloat16)
    vit_own = normalize(hidden, vit_gain)
    vit_rows = lax.all_gather(vit_own, ("head", "sub"), axis=0, tiled=True)
    current = jnp.dot(vit_rows, w_pair[0], preferred_element_type=jnp.float32)
    ahead_proj = jnp.dot(vit_rows, w_pair[1], preferred_element_type=jnp.float32)
    ahead_proj = ahead_proj.reshape(frames_local, cols_local, -1)
    arrived = from_behind(ahead_proj[:1].astype(jnp.bfloat16), "seq", -frame_step).astype(
        jnp.float32
    )
    following = jnp.concatenate([ahead_proj[1:], arrived], axis=0).reshape(block_rows, -1)
    embedded = current + following
    activated = jax.nn.gelu(embedded, approximate=False).reshape(frames_local, cols_local, -1)
    seq_index = lax.axis_index("seq")
    first_token = seq_index * block_rows
    frame_first = first_token // total_cols
    col_first = first_token % total_cols
    patches = total_cols // ROLLS
    roll_ids = (col_first + jnp.arange(cols_local, dtype=jnp.int32)) // patches
    member = (roll_ids[None, :] == jnp.arange(ROLLS, dtype=jnp.int32)[:, None]).astype(
        jnp.float32
    ) / patches
    pooled = jnp.einsum("rp,fpe->fre", member, activated, precision=lax.Precision.HIGHEST)
    scored = jnp.einsum("fre,ea->fra", pooled, w_act, precision=lax.Precision.HIGHEST)
    frame_ids = frame_first + jnp.arange(frames_local, dtype=jnp.int32)
    selector = (pair_frames[:, :, None] == frame_ids[None, None, :]).astype(jnp.float32)
    partial_value = jnp.einsum("rjf,fra->rja", selector, scored, precision=lax.Precision.HIGHEST)
    actions = lax.psum(partial_value, ("seq", "head", "sub"))
    return (hidden, actions)


def solution(mesh):
    in_specs = (
        P(("groups", "seq", "head", "sub"), None),
        P(),
        P(None, ("head", "sub"), None),
        P(("head", "sub"), None),
        P(),
        P(None, None, ("head", "sub")),
        P(("head", "sub"), None),
        P("groups", None),
    )
    out_specs = (P(("groups", "seq", "head", "sub"), None), P("groups", None, None))
    return jax.shard_map(shards, mesh=mesh, in_specs=in_specs, out_specs=out_specs, check_vma=False)
```

profile of v0, /device:TPU:0, one launch (start us, length us, event | category | flops | bytes accessed | tf_op | source)
XLA Modules:
  0.0 155.1 jit_solution(14650567382360925956)
XLA Ops:
  7.2 0.0 copy-start
  7.2 0.0 reduce-scatter.2.cloned.1.call-start
  7.2 1.2 fusion.13
  8.5 1.1 fusion.15
  9.5 10.0 %all_gather.6 = bf16[256,1536]{1,0:T(8,128)(2,1)S(1)} all-gather(bf16[64,1536]{1,0:T(8,128)(2,1)S(1)} %fusion.15), channel_id=1, replica_groups=mesh['groups'=2,'seq'=4,'head'=2,'sub'=2] {'head','sub'}, dimensions={0}, use_global_device_ids=true | all-gather | bytes 983040 | tf_op jit(solution)/shard_map/all_gather | solution.py:36
  19.6 2.1 %convolution_convert_fusion = bf16[256,1152]{1,0:T(8,128)(2,1)} fusion(bf16[256,1536]{1,0:T(8,128)(2,1)S(1)} %all_gather.6, bf16[1536,1152]{0,1:T(8,128)(2,1)S(1)} %bitcast.46), kind=kOutput, calls=%fused_computation.1 | convolution fusion | flops 906264576 | bytes 4915200 | tf_op jit(solution)/shard_map/dot_general | solution.py:37
  21.7 2.8 %reshape.76 = bf16[4,4,16,6,192]{4,3,2,1,0:T(8,128)(2,1)} reshape(bf16[256,1152]{1,0:T(8,128)(2,1)} %convolution_convert_fusion) | data formatting | bytes 1179648 | tf_op jit(solution)/shard_map/reshape | solution.py:38
  24.4 1.4 copy.25
  25.8 25.3 %all_to_all.30 = bf16[4,4,16,6,192]{4,2,3,0,1:T(8,128)(2,1)S(1)} all-to-all(bf16[4,4,16,6,192]{4,2,3,0,1:T(8,128)(2,1)S(1)} %copy.25), channel_id=1, replica_groups=mesh['groups'=2,'seq'=4,'head'=2,'sub'=2] {'seq'}, dimensions={1} | all-to-all | bytes 1179648 | tf_op jit(solution)/shard_map/all_to_all | solution.py:41
  51.1 1.2 fusion.53
  52.4 2.3 %fusion.54 = f32[16,6,16]{2,1,0:T(8,128)} fusion(bf16[16,16,6,64]{3,1,2,0:T(8,128)(2,1)} %get-tuple-element.14, bf16[16,16,6,64]{3,1,2,0:T(8,128)(2,1)} %get-tuple-element.12), kind=kOutput, calls=%fused_computation.79 | convolution fusion | flops 3219471 | bytes 399360 | tf_op jit(solution)/shard_map/sub | solution.py:51
  54.7 2.4 %convolution_multiply_fusion = f32[16,6,16,16]{2,3,1,0:T(8,128)} fusion(bf16[16,16,6,64]{3,1,2,0:T(8,128)(2,1)} %get-tuple-element.14, bf16[16,16,6,64]{3,1,2,0:T(8,128)(2,1)} %get-tuple-element.12), kind=kOutput, calls=%fused_computation.4 | convolution fusion | flops 3170304 | bytes 491520 | tf_op jit(solution)/shard_map/fchd,gchd->chfg/dot_general | solution.py:47
  57.1 2.8 %fusion.3 = bf16[16,16,6,64]{3,0,2,1:T(8,128)(2,1)} fusion(bf16[16,16,6,64]{3,1,2,0:T(8,128)(2,1)} %get-tuple-element.13, f32[16,6,16]{2,1,0:T(8,128)} %fusion.54, f32[16,6,16,16]{2,3,1,0:T(8,128)} %convolution_multiply_fusion), kind=kOutput, calls=%fused_computation.7 | convolution fusion | flops 3319311 | bytes 497664 | tf_op jit(solution)/shard_map/chfg,gchd->fchd/dot_general | solution.py:53
  59.8 1.9 %copy.28 = bf16[16,16,6,64]{3,2,1,0:T(8,128)(2,1)} copy(bf16[16,16,6,64]{3,0,2,1:T(8,128)(2,1)} %fusion.3) | data formatting | bytes 393216 | tf_op jit(solution)/shard_map/convert_element_type | solution.py:55
  61.8 2.1 %reshape.78 = bf16[16,1,16,384]{3,2,0,1:T(8,128)(2,1)} reshape(bf16[16,16,6,64]{3,2,1,0:T(8,128)(2,1)} %copy.28) | data formatting | bytes 393216 | tf_op jit(solution)/shard_map/reshape | solution.py:56
  63.8 10.7 %all_to_all.31 = bf16[16,1,16,384]{3,2,1,0:T(8,128)(2,1)S(1)} all-to-all(bf16[16,1,16,384]{3,2,1,0:T(8,128)(2,1)} %bitcast.51), channel_id=1, replica_groups=mesh['groups'=2,'seq'=4,'head'=2,'sub'=2] {'seq'}, dimensions={0} | all-to-all | bytes 393216 | tf_op jit(solution)/shard_map/all_to_all | solution.py:57
  74.5 2.7 %convolution_convert_fusion.1 = bf16[256,1536]{1,0:T(8,128)(2,1)} fusion(bf16[256,384]{1,0:T(8,128)(2,1)S(1)} %bitcast.48, bf16[384,1536]{1,0:T(8,128)(2,1)} %param.11), kind=kOutput, calls=%fused_computation.2 | convolution fusion | flops 302383104 | bytes 2162688 | tf_op jit(solution)/shard_map/dot_general | solution.py:60
  77.3 0.0 reduce-scatter.2.cloned.1.call-update
  77.3 21.9 %reduce-scatter.2.cloned.1.call-done = bf16[64,1536]{1,0:T(8,128)(2,1)} async-done(((bf16[256,1536]{1,0:T(8,128)(2,1)}), bf16[64,1536]{1,0:T(8,128)(2,1)}) %reduce-scatter.2.cloned.1.call-update) | async-done | bytes 196624 | tf_op jit(solution)/shard_map/reduce_scatter | solution.py:59
  99.2 1.3 fusion.10
  100.6 0.1 fusion.12
  100.7 8.2 %all_gather.7 = bf16[256,1536]{1,0:T(8,128)(2,1)S(1)} all-gather(bf16[64,1536]{1,0:T(8,128)(2,1)S(1)} %fusion.12), channel_id=1, replica_groups=mesh['groups'=2,'seq'=4,'head'=2,'sub'=2] {'head','sub'}, dimensions={0}, use_global_device_ids=true | all-gather | bytes 983040 | tf_op jit(solution)/shard_map/all_gather | solution.py:67
  108.9 0.4 fusion.4
  109.3 1.3 collective-permute-start
  110.6 4.5 %collective-permute-done = bf16[1,64,256]{2,1,0:T(8,128)(2,1)S(1)} collective-permute-done((bf16[1,64,256]{2,1,0:T(8,128)(2,1)S(1)}, bf16[1,64,256]{2,1,0:T(8,128)(2,1)S(1)}, u32[]{:S(2)}, u32[]{:S(2)}) %collective-permute-start) | collective-permute-done | bytes 32800 | tf_op jit(solution)/shard_map/ppermute | solution.py:13
  115.1 0.0 copy-start.3
  115.2 0.9 fusion.22
  116.0 0.3 convolution_bitcast_fusion
  116.3 0.2 fusion.31
  116.5 0.2 fusion.34
  116.7 31.0 %psum.7 = f32[2,15,7]{1,2,0:T(8,128)S(1)} all-reduce(f32[2,15,7]{1,2,0:T(8,128)S(1)} %fusion.34), channel_id=1, replica_groups=mesh['groups'=2,'seq'=4,'head'=2,'sub'=2] {'seq','head','sub'}, use_global_device_ids=true, to_apply=%region_5.6 | all-reduce | flops 210 | bytes 1680 | tf_op jit(solution)/shard_map/psum | solution.py:91
  147.7 0.6 copy.32
  (19 shorter events, 0.1 us)
Async XLA Ops:
  7.2 12.4 %copy-start = (bf16[1536,6,192]{0,2,1:T(8,128)(2,1)S(1)}, bf16[1536,6,192]{0,2,1:T(8,128)(2,1)}, u32[]{:S(2)}) copy-start(bf16[1536,6,192]{0,2,1:T(8,128)(2,1)} %param.10) | copy-start | bytes 10616836
  7.2 92.0 %reduce-scatter.2.cloned.1.call-start = ((), (), s32[]{:S(2)}) async-start(), calls=%async_computation.3 | async-start | bytes 983040 | tf_op jit(solution)/shard_map/reduce_scatter | solution.py:59
  74.5 26.1 %copy-start.2 = (f32[1536]{0:T(1024)S(1)}, f32[1536]{0:T(1024)}, u32[]{:S(2)}) copy-start(f32[1536]{0:T(1024)} %param.12) | copy-start | bytes 18436
  99.2 9.7 %copy-start.4 = (bf16[2,1536,256]{2,1,0:T(8,128)(2,1)S(1)}, bf16[2,1536,256]{2,1,0:T(8,128)(2,1)}, u32[]{:S(2)}) copy-start(bf16[2,1536,256]{2,1,0:T(8,128)(2,1)} %param.13) | copy-start | bytes 4718596
  100.5 8.7 %copy-start.1 = (bf16[64,1536]{1,0:T(8,128)(2,1)}, bf16[64,1536]{1,0:T(8,128)(2,1)S(1)}, u32[]{:S(2)}) copy-start(bf16[64,1536]{1,0:T(8,128)(2,1)S(1)} %get-tuple-element.11) | copy-start | bytes 589828
  109.3 5.8 %collective-permute-start = (bf16[1,64,256]{2,1,0:T(8,128)(2,1)S(1)}, bf16[1,64,256]{2,1,0:T(8,128)(2,1)S(1)}, u32[]{:S(2)}, u32[]{:S(2)}) collective-permute-start(bf16[1,64,256]{2,1,0:T(8,128)(2,1)S(1)} %fusion.30), channel_id=1, source_target_pairs={{4,0},{8,4},{12,8},{5,1},{9,5},{13,9},{6,2},{10,6},{14,10},{7,3},{... | collective-permute-start | bytes 98312 | tf_op jit(solution)/shard_map/ppermute | solution.py:13
  115.1 1.2 copy-start.3
  115.1 1.3 copy-start.5
Sparse Core Ops, SparseCore 0:
  77.4 21.7 reduce-scatter.1
where the time goes:
time: 156 us; the launch traced here: 155 us
  blocking collectives  85.2 us (55%)
  waiting for transfers between devices  26.4 us (17%)
  matrix products  14.2 us (9%)
  between operations  14.2 us (9%)
  local copies, waits for them, and re-layouts  10 us (6%)
  other arithmetic  3.75 us (2%)
    psum x1, blocking collectives, shards(): actions = lax.psum(partial_value, ('seq', 'head', 'sub'))  31 us
    all_to_all x1, blocking collectives, shards(): lax.all_to_all(qkv_rows, 'seq', split_axis=1, concat_axis=0, tiled=True)  25.3 us
    reduce_scatter x1, waiting for transfers between devices, shards(): lax.psum_scatter(jnp.dot(attended, w_out, preferred_element_type=jnp.floa...  21.9 us
    all_to_all x1, blocking collectives, shards(): lax.all_to_all(mixed_out, 'seq', split_axis=0, concat_axis=1, tiled=True)  10.7 us
    all_gather x1, blocking collectives, shards(): lax.all_gather(normalize(frames_in, attn_gain), ('head', 'sub'), axis=0,...  10 us
    all_gather x1, blocking collectives, shards(): vit_rows = lax.all_gather(vit_own, ('head', 'sub'), axis=0, tiled=True)  8.19 us
    ppermute x1, waiting for transfers between devices, from_behind(): lax.ppermute(value, axis, [(source, source + steps) for source in range(l...  4.47 us
    reshape x2, local copies, waits for them, and re-layouts, shards(): qkv_rows.reshape(frames_local, seq_count, cols_local // seq_count, heads_...  4.16 us
  transfers between devices with their start and end apart: 2, of which 2 were waited for; matrix products, arithmetic and copies ran while one was open for 0% of the time, Pallas kernels for 0%

commit v1 on v0

--- a/solution.py
+++ b/solution.py
@@ -1,6 +1,9 @@
+import functools
 import jax
 import jax.numpy as jnp
 from jax import lax
+from jax.experimental import pallas as pl
+from jax.experimental.pallas import tpu as pltpu
 from jax.sharding import PartitionSpec as P
 
 F = 16
@@ -19,7 +22,7 @@
     return (floats * lax.rsqrt(mean_sq + 1e-06) * gain_vec).astype(jnp.bfloat16)
 
 
-def shards(frames_in, attn_gain, w_qkv, w_out, vit_gain, w_pair, w_act, pair_frames):
+def shards_by_frame(frames_in, attn_gain, w_qkv, w_out, vit_gain, w_pair, w_act, pair_frames):
     rows_own = frames_in.shape[0]
     model_width = frames_in.shape[1]
     seq_count = lax.axis_size("seq")
@@ -92,6 +95,444 @@
     return (hidden, actions)
 
 
+def nt_dot(lhs, rhs, **kw):
+    return lax.dot_general(
+        lhs, rhs, (((1,), (1,)), ((), ())), preferred_element_type=jnp.float32, **kw
+    )
+
+
+def tn_dot(lhs, rhs):
+    return lax.dot_general(
+        lhs, rhs, (((0,), (0,)), ((), ())), preferred_element_type=jnp.float32
+    )
+
+
+def fused_kernel(
+    sizes,
+    frames,
+    attn_gain,
+    w_qkv,
+    w_out,
+    vit_gain,
+    w_pair,
+    w_act,
+    pair_frames,
+    hidden_out,
+    actions_out,
+    tokens,
+    normed,
+    wq,
+    wo,
+    wp,
+    mixed,
+    part_send,
+    part_recv,
+    part_own,
+    head_send,
+    head_recv,
+    hidden,
+    vit,
+    pair,
+    scored,
+    local_sem,
+    a_send,
+    a_recv,
+    b_send,
+    b_recv,
+    c_send,
+    c_recv,
+    d_send,
+    d_recv,
+    e_send,
+    e_recv,
+    v_send,
+    v_recv,
+    o_send,
+    o_recv,
+    q_send,
+    q_recv,
+):
+    S, H, U, heads, head_dim = sizes
+    N = S * H * U
+    rows, width = tokens.shape
+    cols = rows // N
+    unit = rows // U
+    chunk = H * cols
+    actions_n, rolls, picks = actions_out.shape
+    out_width = wp.shape[2]
+    s, h, u = lax.axis_index("seq"), lax.axis_index("head"), lax.axis_index("sub")
+    me = (s * H + h) * U + u
+
+    def at(value, size=cols):
+        return pl.ds(pl.multiple_of(value, size), size)
+
+    def slab(u_, s_, h_):
+        return at(((u_ * S + s_) * H + h_) * cols)
+
+    def piece(s_):
+        return at(s_ * chunk, chunk)
+
+    def remote(source, target, send, recv, where):
+        return pltpu.make_async_remote_copy(
+            src_ref=source,
+            dst_ref=target,
+            send_sem=send,
+            recv_sem=recv,
+            device_id=where,
+            device_id_type=pl.DeviceIdType.MESH,
+        )
+
+    sent = []
+
+    def send(*args):
+        copy = remote(*args)
+        copy.start()
+        sent.append(copy)
+
+    load_q = pltpu.make_async_copy(w_qkv, wq, local_sem.at[0])
+    load_o = pltpu.make_async_copy(w_out, wo, local_sem.at[1])
+    load_p = pltpu.make_async_copy(w_pair, wp, local_sem.at[2])
+    load_own = pltpu.make_async_copy(
+        frames.at[at(s * cols)], tokens.at[slab(u, s, h)], local_sem.at[3]
+    )
+    load_own.start()
+    load_q.start()
+    load_o.start()
+    load_p.start()
+
+    barrier = pltpu.get_barrier_semaphore()
+
+    def greet(step, carry):
+        other = lax.rem(me + step, N)
+        where = {"seq": other // (H * U), "head": other // U % H, "sub": other % U}
+        pl.semaphore_signal(
+            barrier, inc=1, device_id=where, device_id_type=pl.DeviceIdType.MESH
+        )
+        return carry
+
+    lax.fori_loop(1, N, greet, 0)
+    pl.semaphore_wait(barrier, N - 1)
+
+    steps = sorted(range(S), key=lambda d: min(d, S - d))
+
+    for dz in reversed(steps[1:]):
+        t = lax.rem(s + dz, S)
+        send(
+            frames.at[at(t * cols)],
+            tokens.at[slab(u, s, h)],
+            a_send.at[dz - 1],
+            a_recv.at[dz - 1],
+            {"seq": t},
+        )
+
+    def to_heads(dz):
+        s_ = lax.rem(s + S - dz, S)
+        place = tokens.at[slab(u, s_, h)]
+        for dh in range(1, H):
+            send(
+                place,
+                place,
+                b_send.at[dh - 1, dz],
+                b_recv.at[dh - 1, dz],
+                {"head": lax.rem(h + dh, H)},
+            )
+        to_subs(0, dz)
+
+    def to_subs(dh, dz):
+        place = tokens.at[slab(u, lax.rem(s + S - dz, S), lax.rem(h + H - dh, H))]
+        for du in range(1, U):
+            send(
+                place,
+                place,
+                c_send.at[du - 1, dh, dz],
+                c_recv.at[du - 1, dh, dz],
+                {"sub": lax.rem(u + du, U)},
+            )
+
+    def from_heads(dz):
+        s_ = lax.rem(s + S - dz, S)
+        for dh in range(1, H):
+            place = tokens.at[slab(u, s_, lax.rem(h + H - dh, H))]
+            remote(
+                place, place, b_send.at[dh - 1, dz], b_recv.at[dh - 1, dz], {"head": h}
+            ).wait_recv()
+            to_subs(dh, dz)
+
+    def scale(values, gain):
+        floats = values.astype(jnp.float32)
+        mean_sq = jnp.mean(floats * floats, axis=-1, keepdims=True)
+        return (floats * lax.rsqrt(mean_sq + 1e-06) * gain[...]).astype(jnp.bfloat16)
+
+    def normalize_piece(u_, s_):
+        place = at((u_ * S + s_) * chunk, chunk)
+        normed[place, :] = scale(tokens[place, :], attn_gain)
+
+    load_own.wait()
+    to_heads(0)
+    for index, dz in enumerate(steps):
+        if index + 1 < S:
+            ahead = steps[index + 1]
+            place = tokens.at[slab(u, lax.rem(s + S - ahead, S), h)]
+            remote(
+                place, place, a_send.at[ahead - 1], a_recv.at[ahead - 1], {"seq": s}
+            ).wait_recv()
+            to_heads(ahead)
+        from_heads(dz)
+        normalize_piece(u, lax.rem(s + S - dz, S))
+    for dz in steps:
+        s_ = lax.rem(s + S - dz, S)
+        for du in range(1, U):
+            u_ = lax.rem(u + U - du, U)
+            for dh in range(H):
+                place = tokens.at[slab(u_, s_, lax.rem(h + H - dh, H))]
+                remote(
+                    place,
+                    place,
+                    c_send.at[du - 1, dh, dz],
+                    c_recv.at[du - 1, dh, dz],
+                    {"sub": u},
+                ).wait_recv()
+            normalize_piece(u_, s_)
+
+    load_q.wait()
+    first = lax.broadcasted_iota(jnp.int32, (rows, rows), 0)
+    second = lax.broadcasted_iota(jnp.int32, (rows, rows), 1)
+    together = lax.rem(first, cols) == lax.rem(second, cols)
+    for head in range(heads):
+        base = head * 3 * head_dim
+        triple = nt_dot(wq[base : base + 3 * head_dim, :], normed[...]).astype(jnp.bfloat16)
+        queries = triple[:head_dim]
+        keys = triple[head_dim : 2 * head_dim]
+        values = triple[2 * head_dim :]
+        scores = jnp.where(together, tn_dot(keys, queries) * head_dim ** (-0.5), -1e30)
+        weights = jnp.exp(scores - jnp.max(scores, axis=0, keepdims=True))
+        total = jnp.sum(weights, axis=0, keepdims=True)
+        out = jnp.dot(values, weights.astype(jnp.bfloat16), preferred_element_type=jnp.float32)
+        mixed[head * head_dim : (head + 1) * head_dim, :] = (out / total).astype(jnp.bfloat16)
+
+    load_o.wait()
+    for du in range(1, U):
+        u_ = lax.rem(u + du, U)
+        block = mixed[:, at(u_ * unit, unit)]
+        part_send[du - 1] = tn_dot(block, wo[...]).astype(jnp.bfloat16)
+        for s_ in range(S):
+            send(
+                part_send.at[du - 1, piece(s_)],
+                part_recv.at[du - 1, piece(s_)],
+                d_send.at[du - 1, s_],
+                d_recv.at[du - 1, s_],
+                {"sub": u_},
+            )
+    part_own[...] = tn_dot(mixed[:, at(u * unit, unit)], wo[...])
+
+    for s_ in range(S):
+        place = piece(s_)
+        value = part_own[place, :]
+        for du in range(1, U):
+            landed = part_recv.at[du - 1, place]
+            remote(
+                landed, landed, d_send.at[du - 1, s_], d_recv.at[du - 1, s_], {"sub": u}
+            ).wait_recv()
+            value = value + part_recv[du - 1, place, :].astype(jnp.float32)
+        part_own[place, :] = value
+        head_send[place, :] = value.astype(jnp.bfloat16)
+        for dh in range(1, H):
+            send(
+                head_send.at[place],
+                head_recv.at[dh - 1, place],
+                e_send.at[dh - 1, s_],
+                e_recv.at[dh - 1, s_],
+                {"head": lax.rem(h + dh, H)},
+            )
+
+    for s_ in range(S):
+        place = piece(s_)
+        whole = at(u * unit + s_ * chunk, chunk)
+        value = part_own[place, :]
+        for dh in range(1, H):
+            landed = head_recv.at[dh - 1, place]
+            remote(
+                landed, landed, e_send.at[dh - 1, s_], e_recv.at[dh - 1, s_], {"head": h}
+            ).wait_recv()
+            value = value + head_recv[dh - 1, place, :].astype(jnp.float32)
+        value = (tokens[whole, :].astype(jnp.float32) + value).astype(jnp.bfloat16)
+        hidden[place, :] = value
+        vit[whole, :] = scale(value, vit_gain)
+        for du in range(1, U):
+            send(
+                vit.at[whole],
+                vit.at[whole],
+                v_send.at[du - 1, s_],
+                v_recv.at[du - 1, s_],
+                {"sub": lax.rem(u + du, U)},
+            )
+        own = hidden.at[at((s_ * H + h) * cols)]
+
+        @pl.when(s_ != s)
+        def _():
+            slot = lax.rem(s_ - s + S, S) - 1
+            remote(
+                own, hidden_out.at[at(s * cols)], o_send.at[slot], o_recv.at[slot], {"seq": s_}
+            ).start()
+
+        @pl.when(s_ == s)
+        def _():
+            pltpu.make_async_copy(own, hidden_out.at[at(s * cols)], local_sem.at[4]).start()
+
+    load_p.wait()
+    for du in range(U):
+        u_ = lax.rem(u + U - du, U)
+        if du:
+            for s_ in range(S):
+                whole = vit.at[at(u_ * unit + s_ * chunk, chunk)]
+                remote(
+                    whole, whole, v_send.at[du - 1, s_], v_recv.at[du - 1, s_], {"sub": u}
+                ).wait_recv()
+        block = vit[at(u_ * unit, unit), :]
+        for side in range(2):
+            pair[side, u_] = jnp.dot(block, wp[side], preferred_element_type=jnp.float32)
+
+    def gelu(x):
+        return 0.5 * x * (1.0 + lax.erf(x * 0.5**0.5))
+
+    pooled = []
+    for u_ in range(U):
+        if u_ + 1 < U:
+            active = gelu(pair[0, u_] + pair[1, u_ + 1])
+        else:
+            active = gelu(pair[0, u_, : unit - cols] + pair[1, 0, cols:])
+            active = jnp.concatenate([active, jnp.zeros((cols, out_width), jnp.float32)], axis=0)
+        pooled.append(jnp.sum(active.reshape(unit // cols, cols, out_width), axis=1))
+    pooled = jnp.concatenate(pooled, axis=0) * (rolls / (cols * S))
+    scored[me, :actions_n, :N] = nt_dot(w_act[...], pooled, precision=lax.Precision.HIGHEST)
+
+    for step in range(1, N):
+        other = lax.rem(me + step, N)
+        where = {"seq": other // (H * U), "head": other // U % H, "sub": other % U}
+        send(scored.at[me], scored.at[me], q_send.at[step - 1], q_recv.at[step - 1], where)
+
+    for dz in range(1, S):
+        s_ = lax.rem(s + dz, S)
+        remote(
+            hidden.at[at((s_ * H + h) * cols)],
+            hidden_out.at[at(s_ * cols)],
+            o_send.at[dz - 1],
+            o_recv.at[dz - 1],
+            {"seq": s},
+        ).wait_send()
+        from_ = lax.rem(s + S - dz, S)
+        remote(
+            hidden.at[at((s_ * H + h) * cols)],
+            hidden_out.at[at(from_ * cols)],
+            o_send.at[dz - 1],
+            o_recv.at[dz - 1],
+            {"seq": s},
+        ).wait_recv()
+    pltpu.make_async_copy(
+        hidden.at[at((s * H + h) * cols)], hidden_out.at[at(s * cols)], local_sem.at[4]
+    ).wait()
+
+    for step in range(1, N):
+        other = lax.rem(me + N - step, N)
+        place = scored.at[other]
+        remote(
+            place, place, q_send.at[step - 1], q_recv.at[step - 1], {"seq": s}
+        ).wait_recv()
+
+    order = lax.broadcasted_iota(jnp.int32, (N, picks), 0)
+    frame = lax.rem(order, S * H) * U + order // (S * H)
+    share = N // rolls
+    for roll in range(rolls):
+        total = scored[roll * share, :actions_n, :N]
+        for index in range(1, share):
+            total = total + scored[roll * share + index, :actions_n, :N]
+        chosen = (frame == pair_frames[roll : roll + 1, :]).astype(jnp.float32)
+        actions_out[:, roll, :] = jnp.dot(
+            total, chosen, preferred_element_type=jnp.float32, precision=lax.Precision.HIGHEST
+        )
+
+    for copy in sent:
+        copy.wait_send()
+
+
+def shards(frames_in, attn_gain, w_qkv, w_out, vit_gain, w_pair, w_act, pair_frames):
+    S, H, U = lax.axis_size("seq"), lax.axis_size("head"), lax.axis_size("sub")
+    N = S * H * U
+    rows_own, width = frames_in.shape
+    heads = w_qkv.shape[1]
+    head_dim = w_qkv.shape[2] // 3
+    out_width = w_pair.shape[2]
+    actions_n = w_act.shape[1]
+    rolls, picks = pair_frames.shape
+    cols = rows_own // S
+    if N != F or rows_own % S or cols % 16 or S % rolls or (H * rows_own) % 128:
+        return shards_by_frame(
+            frames_in, attn_gain, w_qkv, w_out, vit_gain, w_pair, w_act, pair_frames
+        )
+    rows = N * cols
+    unit = rows // U
+    bf16, f32 = jnp.bfloat16, jnp.float32
+    vmem = pl.BlockSpec(memory_space=pltpu.VMEM)
+    anywhere = pl.BlockSpec(memory_space=pl.ANY)
+    dma = pltpu.SemaphoreType.DMA
+    hidden, actions = pl.pallas_call(
+        functools.partial(fused_kernel, (S, H, U, heads, head_dim)),
+        out_shape=(
+            jax.ShapeDtypeStruct((rows_own, width), bf16),
+            jax.ShapeDtypeStruct((actions_n, rolls, picks), f32),
+        ),
+        in_specs=[anywhere, vmem, anywhere, anywhere, vmem, anywhere, vmem, vmem],
+        out_specs=(anywhere, vmem),
+        scratch_shapes=[
+            pltpu.VMEM((rows, width), bf16),
+            pltpu.VMEM((rows, width), bf16),
+            pltpu.VMEM((heads * 3 * head_dim, width), bf16),
+            pltpu.VMEM(w_out.shape, bf16),
+            pltpu.VMEM(w_pair.shape, bf16),
+            pltpu.VMEM((heads * head_dim, rows), bf16),
+            pltpu.VMEM((U - 1, unit, width), bf16),
+            pltpu.VMEM((U - 1, unit, width), bf16),
+            pltpu.VMEM((unit, width), f32),
+            pltpu.VMEM((unit, width), bf16),
+            pltpu.VMEM((H - 1, unit, width), bf16),
+            pltpu.VMEM((unit, width), bf16),
+            pltpu.VMEM((rows, width), bf16),
+            pltpu.VMEM((2, U, unit, out_width), f32),
+            pltpu.VMEM((N, -(-actions_n // 8) * 8, -(-N // 128) * 128), f32),
+            dma((5,)),
+            dma((S - 1,)),
+            dma((S - 1,)),
+            dma((H - 1, S)),
+            dma((H - 1, S)),
+            dma((U - 1, H, S)),
+            dma((U - 1, H, S)),
+            dma((U - 1, S)),
+            dma((U - 1, S)),
+            dma((H - 1, S)),
+            dma((H - 1, S)),
+            dma((U - 1, S)),
+            dma((U - 1, S)),
+            dma((S - 1,)),
+            dma((S - 1,)),
+            dma((N - 1,)),
+            dma((N - 1,)),
+        ],
+        compiler_params=pltpu.CompilerParams(
+            collective_id=0, has_side_effects=True, vmem_limit_bytes=48 * 1024 * 1024
+        ),
+    )(
+        frames_in,
+        attn_gain.reshape(1, width),
+        jnp.transpose(w_qkv, (1, 2, 0)).reshape(heads * 3 * head_dim, width),
+        w_out,
+        vit_gain.reshape(1, width),
+        w_pair,
+        jnp.transpose(w_act, (1, 0)),
+        pair_frames,
+    )
+    return (hidden, jnp.transpose(actions, (1, 2, 0)))
+
+
 def solution(mesh):
     in_specs = (
         P(("groups", "seq", "head", "sub"), None),

time: 156 us -> 50.9 us (0.33)
  blocking collectives: 85.2 us -> 0 us
  Pallas kernels: 0 us -> 42.2 us
  waiting for transfers between devices: 26.4 us -> 0 us
  matrix products: 14.2 us -> 0 us
  between operations: 14.2 us -> 0.64 us
  other arithmetic: 3.75 us -> 0 us
  local copies, waits for them, and re-layouts: 10 us -> 7.65 us
    pallas_call x0 -> x1, Pallas kernels: none -> 42.2 us  [shards(): pl.pallas_call(functools.partial(fused_kernel, (S, H, U, heads, head_dim)...]
    all_to_all x2 -> x0, blocking collectives: 36 us -> none  [the longest x1 25.3 us: shards(): lax.all_to_all(qkv_rows, 'seq', split_axis=1, concat_axis=0, tiled=True)]
    psum x1 -> x0, blocking collectives: 31 us -> none  [shards(): actions = lax.psum(partial_value, ('seq', 'head', 'sub'))]
    reduce_scatter x1 -> x0, waiting for transfers between devices: 21.9 us -> none  [shards(): lax.psum_scatter(jnp.dot(attended, w_out, preferred_element_type=jnp.floa...]
    all_gather x2 -> x0, blocking collectives: 18.2 us -> none  [the longest x1 10 us: shards(): lax.all_gather(normalize(frames_in, attn_gain), ('head', 'sub'), axis=0,...]
    dot_general x9 -> x0, matrix products: 11.8 us -> none  [the longest x1 2.75 us: shards(): jnp.einsum('chfg,gchd->fchd', weights, value_part, preferred_element_type...]
    unnamed x13 -> x12, local copies, waits for them, and re-layouts: 0.64 us -> 6.25 us
    reshape x3 -> x2, local copies, waits for them, and re-layouts: 6.22 us -> 1.4 us  [the longest x1 0.7 us: shards(): attn_gain.reshape(1, width)]
  transfers between devices with their start and end apart: 2 -> 0, of which waited for: 2 -> 0; matrix products, arithmetic and copies ran while one was open for 0% -> 0% of each run, Pallas kernels for 0% -> 0%
where the time goes in v1:
time: 50.9 us; the launch traced here: 50.5 us
  Pallas kernels  42.2 us (83%)
  local copies, waits for them, and re-layouts  7.65 us (15%)
  between operations  0.64 us (1%)
    pallas_call x1, Pallas kernels, shards(): pl.pallas_call(functools.partial(fused_kernel, (S, H, U, heads, head_dim)...  42.2 us
    unnamed x12, local copies, waits for them, and re-layouts  6.25 us

profile of v1, /device:TPU:0, one launch (start us, length us, event | category | flops | bytes accessed | tf_op | source)
XLA Modules:
  0.0 50.5 jit_solution(9306760529322269144)
XLA Ops:
  0.6 0.7 %reshape.13.attn_gain = f32[1,1536]{1,0:T(1,128)S(1)} reshape(f32[1536]{0:T(1024)} %param.9) | data formatting | bytes 12288 | tf_op jit(solution)/shard_map/reshape | solution.py:525
  1.3 0.7 %reshape.15.vit_gain = f32[1,1536]{1,0:T(1,128)S(1)} reshape(f32[1536]{0:T(1024)} %param.12) | data formatting | bytes 12288 | tf_op jit(solution)/shard_map/reshape | solution.py:528
  2.0 0.0 copy-start
  2.0 1.4 %copy-done = bf16[2,1536,256]{2,1,0:T(8,128)(2,1)S(1)} copy-done((bf16[2,1536,256]{2,1,0:T(8,128)(2,1)S(1)}, bf16[2,1536,256]{2,1,0:T(8,128)(2,1)}, u32[]{:S(2)}) %copy-start) | copy-done | bytes 1572888
  3.4 0.0 copy-start.1
  3.4 1.3 %copy-done.1 = bf16[384,1536]{1,0:T(8,128)(2,1)S(1)} copy-done((bf16[384,1536]{1,0:T(8,128)(2,1)S(1)}, bf16[384,1536]{1,0:T(8,128)(2,1)}, u32[]{:S(2)}) %copy-start.1) | copy-done | bytes 1179672
  4.7 0.0 copy-start.2
  4.7 0.9 %copy-done.2 = bf16[64,1536]{1,0:T(8,128)(2,1)S(1)} copy-done((bf16[64,1536]{1,0:T(8,128)(2,1)S(1)}, bf16[64,1536]{1,0:T(8,128)(2,1)}, u32[]{:S(2)}) %copy-start.2) | copy-done | bytes 196632
  5.6 0.0 copy-start.3
  5.6 0.7 %copy-done.3 = f32[256,7]{0,1:T(8,128)S(1)} copy-done((f32[256,7]{0,1:T(8,128)S(1)}, f32[256,7]{0,1:T(8,128)}, u32[]{:S(2)}) %copy-start.3) | copy-done | bytes 7192
  6.3 0.0 copy-start.4
  6.3 0.7 %copy-done.4 = s32[2,15]{1,0:T(2,128)S(1)} copy-done((s32[2,15]{1,0:T(2,128)S(1)}, s32[2,15]{1,0:T(2,128)}, u32[]{:S(2)}) %copy-start.4) | copy-done | bytes 144
  7.0 42.2 %shard_map.95 = (bf16[64,1536]{1,0:T(8,128)(2,1)S(1)}, f32[7,2,15]{2,1,0:T(2,128)S(1)}) custom-call(bf16[64,1536]{1,0:T(8,128)(2,1)S(1)} %copy-done.2, f32[1,1536]{1,0:T(1,128)S(1)} %reshape.13.attn_gain, bf16[1152,1536]{1,0:T(8,128)(2,1)} %bitcast.7, bf16[384,1536]{1,0:T(8,128)(2,1)S(1)} %copy-done.1, f32[1,1536]{1,0:T(1,128)S(1)} %reshape.15.vit_gain, ...), custom_call_target="tpu_custom_call" | custom-call | tf_op jit(solution)/shard_map/pallas_call | solution.py:478
  49.2 0.7 %copy.12 = bf16[64,1536]{1,0:T(8,128)(2,1)} copy(bf16[64,1536]{1,0:T(8,128)(2,1)S(1)} %get-tuple-element.8) | data formatting | bytes 393216
  49.9 0.6 %copy.13 = f32[2,15,7]{1,0,2:T(2,128)} copy(f32[2,15,7]{1,0,2:T(2,128)S(1)} %bitcast.6) | data formatting | bytes 1680
Async XLA Ops:
  2.0 1.4 %copy-start = (bf16[2,1536,256]{2,1,0:T(8,128)(2,1)S(1)}, bf16[2,1536,256]{2,1,0:T(8,128)(2,1)}, u32[]{:S(2)}) copy-start(bf16[2,1536,256]{2,1,0:T(8,128)(2,1)} %w_pair.1) | copy-start | bytes 4718596
  3.4 1.3 %copy-start.1 = (bf16[384,1536]{1,0:T(8,128)(2,1)S(1)}, bf16[384,1536]{1,0:T(8,128)(2,1)}, u32[]{:S(2)}) copy-start(bf16[384,1536]{1,0:T(8,128)(2,1)} %w_out.1) | copy-start | bytes 3538948
  4.7 0.9 %copy-start.2 = (bf16[64,1536]{1,0:T(8,128)(2,1)S(1)}, bf16[64,1536]{1,0:T(8,128)(2,1)}, u32[]{:S(2)}) copy-start(bf16[64,1536]{1,0:T(8,128)(2,1)} %frames.1) | copy-start | bytes 589828
  5.6 0.7 %copy-start.3 = (f32[256,7]{0,1:T(8,128)S(1)}, f32[256,7]{0,1:T(8,128)}, u32[]{:S(2)}) copy-start(f32[256,7]{0,1:T(8,128)} %param.14) | copy-start | bytes 21508
  6.3 0.7 %copy-start.4 = (s32[2,15]{1,0:T(2,128)S(1)}, s32[2,15]{1,0:T(2,128)}, u32[]{:S(2)}) copy-start(s32[2,15]{1,0:T(2,128)} %pair_frames.1) | copy-start | bytes 364

commit v2 on v1

--- a/solution.py
+++ b/solution.py
@@ -110,15 +110,19 @@
 def fused_kernel(
     sizes,
     frames,
-    attn_gain,
+    attn_gain_in,
     w_qkv,
     w_out,
+    vit_gain_in,
+    w_pair,
+    w_act_in,
+    pair_frames_in,
+    hidden_out,
+    actions_out,
+    attn_gain,
     vit_gain,
-    w_pair,
     w_act,
     pair_frames,
-    hidden_out,
-    actions_out,
     tokens,
     normed,
     wq,
@@ -195,7 +199,20 @@
     load_own = pltpu.make_async_copy(
         frames.at[at(s * cols)], tokens.at[slab(u, s, h)], local_sem.at[3]
     )
+    small = [
+        pltpu.make_async_copy(source, target, local_sem.at[5 + index])
+        for index, (source, target) in enumerate(
+            (
+                (attn_gain_in, attn_gain),
+                (vit_gain_in, vit_gain),
+                (w_act_in, w_act),
+                (pair_frames_in, pair_frames),
+            )
+        )
+    ]
     load_own.start()
+    for load in small:
+        load.start()
     load_q.start()
     load_o.start()
     load_p.start()
@@ -261,7 +278,7 @@
     def scale(values, gain):
         floats = values.astype(jnp.float32)
         mean_sq = jnp.mean(floats * floats, axis=-1, keepdims=True)
-        return (floats * lax.rsqrt(mean_sq + 1e-06) * gain[...]).astype(jnp.bfloat16)
+        return (floats * lax.rsqrt(mean_sq + 1e-06) * gain[...][None, :]).astype(jnp.bfloat16)
 
     def normalize_piece(u_, s_):
         place = at((u_ * S + s_) * chunk, chunk)
@@ -269,6 +286,8 @@
 
     load_own.wait()
     to_heads(0)
+    for load in small:
+        load.wait()
     for index, dz in enumerate(steps):
         if index + 1 < S:
             ahead = steps[index + 1]
@@ -481,9 +500,13 @@
             jax.ShapeDtypeStruct((rows_own, width), bf16),
             jax.ShapeDtypeStruct((actions_n, rolls, picks), f32),
         ),
-        in_specs=[anywhere, vmem, anywhere, anywhere, vmem, anywhere, vmem, vmem],
+        in_specs=[anywhere] * 8,
         out_specs=(anywhere, vmem),
         scratch_shapes=[
+            pltpu.VMEM((width,), f32),
+            pltpu.VMEM((width,), f32),
+            pltpu.VMEM((actions_n, out_width), f32),
+            pltpu.VMEM((rolls, picks), jnp.int32),
             pltpu.VMEM((rows, width), bf16),
             pltpu.VMEM((rows, width), bf16),
             pltpu.VMEM((heads * 3 * head_dim, width), bf16),
@@ -499,7 +522,7 @@
             pltpu.VMEM((rows, width), bf16),
             pltpu.VMEM((2, U, unit, out_width), f32),
             pltpu.VMEM((N, -(-actions_n // 8) * 8, -(-N // 128) * 128), f32),
-            dma((5,)),
+            dma((9,)),
             dma((S - 1,)),
             dma((S - 1,)),
             dma((H - 1, S)),
@@ -518,14 +541,14 @@
             dma((N - 1,)),
         ],
         compiler_params=pltpu.CompilerParams(
-            collective_id=0, has_side_effects=True, vmem_limit_bytes=48 * 1024 * 1024
+            collective_id=0, has_side_effects=True, vmem_limit_bytes=60 * 1024 * 1024
         ),
     )(
         frames_in,
-        attn_gain.reshape(1, width),
+        attn_gain,
         jnp.transpose(w_qkv, (1, 2, 0)).reshape(heads * 3 * head_dim, width),
         w_out,
-        vit_gain.reshape(1, width),
+        vit_gain,
         w_pair,
         jnp.transpose(w_act, (1, 0)),
         pair_frames,

time: 50.9 us -> 46.4 us (0.912)
  local copies, waits for them, and re-layouts: 7.65 us -> 2.9 us
    unnamed x12 -> x2, local copies, waits for them, and re-layouts: 6.25 us -> 2.9 us
    reshape x2 -> x0, local copies, waits for them, and re-layouts: 1.4 us -> none  [the longest x1 0.7 us: shards(): attn_gain.reshape(1, width)]
where the time goes in v2:
time: 46.4 us; the launch traced here: 46.3 us
  Pallas kernels  42.7 us (92%)
  local copies, waits for them, and re-layouts  2.9 us (6%)
  between operations  0.64 us (1%)
    pallas_call x1, Pallas kernels, shards(): pl.pallas_call(functools.partial(fused_kernel, (S, H, U, heads, head_dim)...  42.7 us
    unnamed x2, local copies, waits for them, and re-layouts  2.9 us

profile of v2, /device:TPU:0, one launch (start us, length us, event | category | flops | bytes accessed | tf_op | source)
XLA Modules:
  0.0 46.3 jit_solution(5907466536654827949)
XLA Ops:
  0.6 42.7 %shard_map.95 = (bf16[64,1536]{1,0:T(8,128)(2,1)}, f32[7,2,15]{2,1,0:T(2,128)}) custom-call(bf16[64,1536]{1,0:T(8,128)(2,1)} %frames.1, f32[1536]{0:T(1024)} %attn_gain_in.1, bf16[1152,1536]{1,0:T(8,128)(2,1)} %bitcast.5, bf16[384,1536]{1,0:T(8,128)(2,1)} %w_out.1, f32[1536]{0:T(1024)} %vit_gain_in.1, bf16[2,1536,256]{2,1,0:T(8,128)(2,1)} %w_pair.1, ...), custom_call_target="tpu_custom_call" | custom-call | tf_op jit(solution)/shard_map/pallas_call | solution.py:497
  43.3 1.6 %copy.12 = bf16[64,1536]{1,0:T(8,128)(2,1)} copy(bf16[64,1536]{1,0:T(8,128)(2,1)} %get-tuple-element.8) | data formatting | bytes 393216
  45.0 1.3 %copy.13 = f32[2,15,7]{1,0,2:T(2,128)} copy(f32[2,15,7]{1,0,2:T(2,128)} %bitcast.7) | data formatting | bytes 1680

commit v3 on v2

--- a/solution.py
+++ b/solution.py
@@ -95,6 +95,10 @@
     return (hidden, actions)
 
 
+HALVES = 2
+PIECES = 2
+
+
 def nt_dot(lhs, rhs, **kw):
     return lax.dot_general(
         lhs, rhs, (((1,), (1,)), ((), ())), preferred_element_type=jnp.float32, **kw
@@ -128,15 +132,17 @@
     wq,
     wo,
     wp,
+    qkv,
     mixed,
+    branch,
     part_send,
     part_recv,
     part_own,
     head_send,
     head_recv,
+    hidden_wide,
     hidden,
     vit,
-    pair,
     scored,
     local_sem,
     a_send,
@@ -162,6 +168,12 @@
     cols = rows // N
     unit = rows // U
     chunk = H * cols
+    part = cols // HALVES
+    half_rows = rows // HALVES
+    half_unit = unit // HALVES
+    pieces = HALVES * PIECES
+    piece_rows = half_unit // PIECES
+    piece_seq = S // PIECES
     actions_n, rolls, picks = actions_out.shape
     out_width = wp.shape[2]
     s, h, u = lax.axis_index("seq"), lax.axis_index("head"), lax.axis_index("sub")
@@ -173,8 +185,16 @@
     def slab(u_, s_, h_):
         return at(((u_ * S + s_) * H + h_) * cols)
 
-    def piece(s_):
-        return at(s_ * chunk, chunk)
+    def piece(p):
+        return at(p * piece_rows, piece_rows)
+
+    def vit_piece(u_, p):
+        half, index = divmod(p, PIECES)
+        start = half * half_rows + u_ * half_unit + index * piece_rows
+        return at(start, piece_rows)
+
+    def halved(values, half):
+        return values.reshape(-1, HALVES, part, width)[:, half].reshape(-1, width)
 
     def remote(source, target, send, recv, where):
         return pltpu.make_async_remote_copy(
@@ -278,11 +298,14 @@
     def scale(values, gain):
         floats = values.astype(jnp.float32)
         mean_sq = jnp.mean(floats * floats, axis=-1, keepdims=True)
-        return (floats * lax.rsqrt(mean_sq + 1e-06) * gain[...][None, :]).astype(jnp.bfloat16)
+        return floats * lax.rsqrt(mean_sq + 1e-06) * gain[...][None, :]
 
     def normalize_piece(u_, s_):
         place = at((u_ * S + s_) * chunk, chunk)
-        normed[place, :] = scale(tokens[place, :], attn_gain)
+        scaled = scale(tokens[place, :], attn_gain)
+        for half in range(HALVES):
+            target = at(half * half_rows + (u_ * S + s_) * H * part, H * part)
+            normed[target, :] = halved(scaled, half).astype(jnp.bfloat16)
 
     load_own.wait()
     to_heads(0)
@@ -314,78 +337,115 @@
             normalize_piece(u_, s_)
 
     load_q.wait()
-    first = lax.broadcasted_iota(jnp.int32, (rows, rows), 0)
-    second = lax.broadcasted_iota(jnp.int32, (rows, rows), 1)
-    together = lax.rem(first, cols) == lax.rem(second, cols)
-    for head in range(heads):
+    first = lax.broadcasted_iota(jnp.int32, (half_rows, half_rows), 0)
+    second = lax.broadcasted_iota(jnp.int32, (half_rows, half_rows), 1)
+    together = lax.rem(first, part) == lax.rem(second, part)
+
+    def project(head):
         base = head * 3 * head_dim
-        triple = nt_dot(wq[base : base + 3 * head_dim, :], normed[...]).astype(jnp.bfloat16)
-        queries = triple[:head_dim]
-        keys = triple[head_dim : 2 * head_dim]
-        values = triple[2 * head_dim :]
+        qkv[base : base + 3 * head_dim, :] = nt_dot(
+            wq[base : base + 3 * head_dim, :], normed[...]
+        ).astype(jnp.bfloat16)
+
+    def attend(head, half):
+        base = head * 3 * head_dim
+        lanes = slice(half * half_rows, (half + 1) * half_rows)
+        queries = qkv[base : base + head_dim, lanes]
+        keys = qkv[base + head_dim : base + 2 * head_dim, lanes]
+        values = qkv[base + 2 * head_dim : base + 3 * head_dim, lanes]
         scores = jnp.where(together, tn_dot(keys, queries) * head_dim ** (-0.5), -1e30)
         weights = jnp.exp(scores - jnp.max(scores, axis=0, keepdims=True))
         total = jnp.sum(weights, axis=0, keepdims=True)
         out = jnp.dot(values, weights.astype(jnp.bfloat16), preferred_element_type=jnp.float32)
-        mixed[head * head_dim : (head + 1) * head_dim, :] = (out / total).astype(jnp.bfloat16)
-
+        mixed[head * head_dim : (head + 1) * head_dim, lanes] = (out / total).astype(jnp.bfloat16)
+
+    def output(half):
+        lanes = slice(half * half_rows, (half + 1) * half_rows)
+        branch[half] = tn_dot(mixed[:, lanes], wo[...])
+        for du in range(1, U):
+            u_ = lax.rem(u + du, U)
+            for p in range(half * PIECES, (half + 1) * PIECES):
+                start = u_ * half_unit + (p % PIECES) * piece_rows
+                part_send[du - 1, piece(p), :] = branch[half, at(start, piece_rows), :].astype(
+                    jnp.bfloat16
+                )
+                send(
+                    part_send.at[du - 1, piece(p)],
+                    part_recv.at[du - 1, piece(p)],
+                    d_send.at[du - 1, p],
+                    d_recv.at[du - 1, p],
+                    {"sub": u_},
+                )
+
+    def exchange(half):
+        for p in range(half * PIECES, (half + 1) * PIECES):
+            place = piece(p)
+            start = u * half_unit + (p % PIECES) * piece_rows
+            value = branch[half, at(start, piece_rows), :]
+            for du in range(1, U):
+                landed = part_recv.at[du - 1, place]
+                remote(
+                    landed, landed, d_send.at[du - 1, p], d_recv.at[du - 1, p], {"sub": u}
+                ).wait_recv()
+                value = value + part_recv[du - 1, place, :].astype(jnp.float32)
+            part_own[place, :] = value
+            head_send[place, :] = value.astype(jnp.bfloat16)
+            for dh in range(1, H):
+                send(
+                    head_send.at[place],
+                    head_recv.at[dh - 1, place],
+                    e_send.at[dh - 1, p],
+                    e_recv.at[dh - 1, p],
+                    {"head": lax.rem(h + dh, H)},
+                )
+
+    for head in range(heads):
+        project(head)
+        attend(head, 0)
     load_o.wait()
-    for du in range(1, U):
-        u_ = lax.rem(u + du, U)
-        block = mixed[:, at(u_ * unit, unit)]
-        part_send[du - 1] = tn_dot(block, wo[...]).astype(jnp.bfloat16)
-        for s_ in range(S):
-            send(
-                part_send.at[du - 1, piece(s_)],
-                part_recv.at[du - 1, piece(s_)],
-                d_send.at[du - 1, s_],
-                d_recv.at[du - 1, s_],
-                {"sub": u_},
-            )
-    part_own[...] = tn_dot(mixed[:, at(u * unit, unit)], wo[...])
-
-    for s_ in range(S):
-        place = piece(s_)
-        value = part_own[place, :]
-        for du in range(1, U):
-            landed = part_recv.at[du - 1, place]
-            remote(
-                landed, landed, d_send.at[du - 1, s_], d_recv.at[du - 1, s_], {"sub": u}
-            ).wait_recv()
-            value = value + part_recv[du - 1, place, :].astype(jnp.float32)
-        part_own[place, :] = value
-        head_send[place, :] = value.astype(jnp.bfloat16)
-        for dh in range(1, H):
-            send(
-                head_send.at[place],
-                head_recv.at[dh - 1, place],
-                e_send.at[dh - 1, s_],
-                e_recv.at[dh - 1, s_],
-                {"head": lax.rem(h + dh, H)},
-            )
-
-    for s_ in range(S):
-        place = piece(s_)
-        whole = at(u * unit + s_ * chunk, chunk)
+    output(0)
+    for half in range(1, HALVES):
+        for head in range(heads // 2):
+            attend(head, half)
+        exchange(half - 1)
+        for head in range(heads // 2, heads):
+            attend(head, half)
+        output(half)
+    exchange(HALVES - 1)
+
+    def finish(p):
+        half, index = divmod(p, PIECES)
+        place = piece(p)
         value = part_own[place, :]
         for dh in range(1, H):
             landed = head_recv.at[dh - 1, place]
             remote(
-                landed, landed, e_send.at[dh - 1, s_], e_recv.at[dh - 1, s_], {"head": h}
+                landed, landed, e_send.at[dh - 1, p], e_recv.at[dh - 1, p], {"head": h}
             ).wait_recv()
             value = value + head_recv[dh - 1, place, :].astype(jnp.float32)
-        value = (tokens[whole, :].astype(jnp.float32) + value).astype(jnp.bfloat16)
-        hidden[place, :] = value
-        vit[whole, :] = scale(value, vit_gain)
+        block = piece_rows * HALVES
+        source = at(u * unit + index * block, block)
+        value = value + halved(tokens[source, :].astype(jnp.float32), half)
+        value = value.astype(jnp.bfloat16)
+        wide = value.astype(jnp.float32)
+        hidden_wide[half, index * piece_seq : (index + 1) * piece_seq] = wide.reshape(
+            piece_seq, H, part, width
+        )
+        mine = vit_piece(u, p)
+        vit[mine, :] = scale(value, vit_gain).astype(jnp.bfloat16)
         for du in range(1, U):
             send(
-                vit.at[whole],
-                vit.at[whole],
-                v_send.at[du - 1, s_],
-                v_recv.at[du - 1, s_],
+                vit.at[mine],
+                vit.at[mine],
+                v_send.at[du - 1, p],
+                v_recv.at[du - 1, p],
                 {"sub": lax.rem(u + du, U)},
             )
-        own = hidden.at[at((s_ * H + h) * cols)]
+
+    def send_hidden(s_):
+        rows_ = [hidden_wide[half, s_, h] for half in range(HALVES)]
+        hidden[s_] = jnp.concatenate(rows_, axis=0).astype(jnp.bfloat16)
+        own = hidden.at[s_]
 
         @pl.when(s_ != s)
         def _():
@@ -398,31 +458,41 @@
         def _():
             pltpu.make_async_copy(own, hidden_out.at[at(s * cols)], local_sem.at[4]).start()
 
-    load_p.wait()
-    for du in range(U):
-        u_ = lax.rem(u + U - du, U)
-        if du:
-            for s_ in range(S):
-                whole = vit.at[at(u_ * unit + s_ * chunk, chunk)]
-                remote(
-                    whole, whole, v_send.at[du - 1, s_], v_recv.at[du - 1, s_], {"sub": u}
-                ).wait_recv()
-        block = vit[at(u_ * unit, unit), :]
-        for side in range(2):
-            pair[side, u_] = jnp.dot(block, wp[side], preferred_element_type=jnp.float32)
-
     def gelu(x):
         return 0.5 * x * (1.0 + lax.erf(x * 0.5**0.5))
 
-    pooled = []
-    for u_ in range(U):
-        if u_ + 1 < U:
-            active = gelu(pair[0, u_] + pair[1, u_ + 1])
-        else:
-            active = gelu(pair[0, u_, : unit - cols] + pair[1, 0, cols:])
-            active = jnp.concatenate([active, jnp.zeros((cols, out_width), jnp.float32)], axis=0)
-        pooled.append(jnp.sum(active.reshape(unit // cols, cols, out_width), axis=1))
-    pooled = jnp.concatenate(pooled, axis=0) * (rolls / (cols * S))
+    def embed(half):
+        for du in range(1, U):
+            for p in range(half * PIECES, (half + 1) * PIECES):
+                theirs = vit.at[vit_piece(lax.rem(u + U - du, U), p)]
+                remote(
+                    theirs, theirs, v_send.at[du - 1, p], v_recv.at[du - 1, p], {"sub": u}
+                ).wait_recv()
+        block = vit[half * half_rows : (half + 1) * half_rows, :]
+        now = jnp.dot(block, wp[0], preferred_element_type=jnp.float32)
+        then = jnp.dot(block, wp[1], preferred_element_type=jnp.float32)
+        pooled = []
+        for u_ in range(U):
+            start, stop = u_ * half_unit, (u_ + 1) * half_unit
+            if u_ + 1 < U:
+                active = gelu(now[start:stop] + then[stop : stop + half_unit])
+            else:
+                active = gelu(now[start : stop - part] + then[part:half_unit])
+                active = jnp.concatenate([active, jnp.zeros((part, out_width), jnp.float32)], axis=0)
+            pooled.append(jnp.sum(active.reshape(-1, part, out_width), axis=1))
+        return jnp.concatenate(pooled, axis=0)
+
+    load_p.wait()
+    pooled = jnp.zeros((N, out_width), jnp.float32)
+    for half in range(HALVES):
+        for p in range(half * PIECES, (half + 1) * PIECES):
+            finish(p)
+            if half == HALVES - 1:
+                index = p % PIECES
+                for s_ in range(index * piece_seq, (index + 1) * piece_seq):
+                    send_hidden(s_)
+        pooled = pooled + embed(half)
+    pooled = pooled * (rolls / (cols * S))
     scored[me, :actions_n, :N] = nt_dot(w_act[...], pooled, precision=lax.Precision.HIGHEST)
 
     for step in range(1, N):
@@ -433,7 +503,7 @@
     for dz in range(1, S):
         s_ = lax.rem(s + dz, S)
         remote(
-            hidden.at[at((s_ * H + h) * cols)],
+            hidden.at[s_],
             hidden_out.at[at(s_ * cols)],
             o_send.at[dz - 1],
             o_recv.at[dz - 1],
@@ -441,14 +511,14 @@
         ).wait_send()
         from_ = lax.rem(s + S - dz, S)
         remote(
-            hidden.at[at((s_ * H + h) * cols)],
+            hidden.at[s_],
             hidden_out.at[at(from_ * cols)],
             o_send.at[dz - 1],
             o_recv.at[dz - 1],
             {"seq": s},
         ).wait_recv()
     pltpu.make_async_copy(
-        hidden.at[at((s * H + h) * cols)], hidden_out.at[at(s * cols)], local_sem.at[4]
+        hidden.at[s], hidden_out.at[at(s * cols)], local_sem.at[4]
     ).wait()
 
     for step in range(1, N):
@@ -484,7 +554,8 @@
     actions_n = w_act.shape[1]
     rolls, picks = pair_frames.shape
     cols = rows_own // S
-    if N != F or rows_own % S or cols % 16 or S % rolls or (H * rows_own) % 128:
+    whole = rows_own % S == 0 and cols % 16 == 0 and S % rolls == 0 and S % PIECES == 0
+    if N != F or not whole or (H * rows_own) % 128 or (H * U * rows_own) % (128 * HALVES):
         return shards_by_frame(
             frames_in, attn_gain, w_qkv, w_out, vit_gain, w_pair, w_act, pair_frames
         )
@@ -512,15 +583,17 @@
             pltpu.VMEM((heads * 3 * head_dim, width), bf16),
             pltpu.VMEM(w_out.shape, bf16),
             pltpu.VMEM(w_pair.shape, bf16),
+            pltpu.VMEM((heads * 3 * head_dim, rows), bf16),
             pltpu.VMEM((heads * head_dim, rows), bf16),
+            pltpu.VMEM((HALVES, rows // HALVES, width), f32),
             pltpu.VMEM((U - 1, unit, width), bf16),
             pltpu.VMEM((U - 1, unit, width), bf16),
             pltpu.VMEM((unit, width), f32),
             pltpu.VMEM((unit, width), bf16),
             pltpu.VMEM((H - 1, unit, width), bf16),
-            pltpu.VMEM((unit, width), bf16),
+            pltpu.VMEM((HALVES, S, H, cols // HALVES, width), f32),
+            pltpu.VMEM((S, cols, width), bf16),
             pltpu.VMEM((rows, width), bf16),
-            pltpu.VMEM((2, U, unit, out_width), f32),
             pltpu.VMEM((N, -(-actions_n // 8) * 8, -(-N // 128) * 128), f32),
             dma((9,)),
             dma((S - 1,)),
@@ -529,12 +602,12 @@
             dma((H - 1, S)),
             dma((U - 1, H, S)),
             dma((U - 1, H, S)),
-            dma((U - 1, S)),
-            dma((U - 1, S)),
-            dma((H - 1, S)),
-            dma((H - 1, S)),
-            dma((U - 1, S)),
-            dma((U - 1, S)),
+            dma((U - 1, HALVES * PIECES)),
+            dma((U - 1, HALVES * PIECES)),
+            dma((H - 1, HALVES * PIECES)),
+            dma((H - 1, HALVES * PIECES)),
+            dma((U - 1, HALVES * PIECES)),
+            dma((U - 1, HALVES * PIECES)),
             dma((S - 1,)),
             dma((S - 1,)),
             dma((N - 1,)),

time: 46.4 us -> 45.8 us (0.987)
  Pallas kernels: 42.7 us -> 42.1 us
    pallas_call x1, Pallas kernels: 42.7 us -> 42.1 us  [shards(): pl.pallas_call(functools.partial(fused_kernel, (S, H, U, heads, head_dim)...]
where the time goes in v3:
time: 45.8 us; the launch traced here: 45.6 us
  Pallas kernels  42.1 us (92%)
  local copies, waits for them, and re-layouts  2.9 us (6%)
  between operations  0.64 us (1%)
    pallas_call x1, Pallas kernels, shards(): pl.pallas_call(functools.partial(fused_kernel, (S, H, U, heads, head_dim)...  42.1 us
    unnamed x2, local copies, waits for them, and re-layouts  2.9 us

profile of v3, /device:TPU:0, one launch (start us, length us, event | category | flops | bytes accessed | tf_op | source)
XLA Modules:
  0.0 45.6 jit_solution(1439043436428275176)
XLA Ops:
  0.6 42.1 %shard_map.95 = (bf16[64,1536]{1,0:T(8,128)(2,1)}, f32[7,2,15]{2,1,0:T(2,128)}) custom-call(bf16[64,1536]{1,0:T(8,128)(2,1)} %frames.1, f32[1536]{0:T(1024)} %attn_gain_in.1, bf16[1152,1536]{1,0:T(8,128)(2,1)} %bitcast.5, bf16[384,1536]{1,0:T(8,128)(2,1)} %w_out.1, f32[1536]{0:T(1024)} %vit_gain_in.1, bf16[2,1536,256]{2,1,0:T(8,128)(2,1)} %w_pair.1, ...), custom_call_target="tpu_custom_call" | custom-call | tf_op jit(solution)/shard_map/pallas_call | solution.py:568
  42.7 1.6 %copy.12 = bf16[64,1536]{1,0:T(8,128)(2,1)} copy(bf16[64,1536]{1,0:T(8,128)(2,1)} %get-tuple-element.8) | data formatting | bytes 393216
  44.4 1.3 %copy.13 = f32[2,15,7]{1,0,2:T(2,128)} copy(f32[2,15,7]{1,0,2:T(2,128)} %bitcast.7) | data formatting | bytes 1680

commit v4 on v3

--- a/solution.py
+++ b/solution.py
@@ -127,6 +127,8 @@
     vit_gain,
     w_act,
     pair_frames,
+    own_frames,
+    outgoing,
     tokens,
     normed,
     wq,
@@ -164,10 +166,10 @@
 ):
     S, H, U, heads, head_dim = sizes
     N = S * H * U
-    rows, width = tokens.shape
+    width = wq.shape[1]
+    rows = mixed.shape[1]
     cols = rows // N
     unit = rows // U
-    chunk = H * cols
     part = cols // HALVES
     half_rows = rows // HALVES
     half_unit = unit // HALVES
@@ -182,8 +184,11 @@
     def at(value, size=cols):
         return pl.ds(pl.multiple_of(value, size), size)
 
-    def slab(u_, s_, h_):
-        return at(((u_ * S + s_) * H + h_) * cols)
+    def order(u_, s_, h_):
+        return (u_ * S + s_) * H + h_
+
+    def behind(d):
+        return lax.rem(s + S - d, S)
 
     def piece(p):
         return at(p * piece_rows, piece_rows)
@@ -193,8 +198,11 @@
         start = half * half_rows + u_ * half_unit + index * piece_rows
         return at(start, piece_rows)
 
-    def halved(values, half):
-        return values.reshape(-1, HALVES, part, width)[:, half].reshape(-1, width)
+    def unpack(half, start, count):
+        packed = tokens[half, pl.ds(start, count)].astype(jnp.float32)
+        packed = packed.reshape(count, HALVES, part, width // HALVES)
+        wide = jnp.concatenate([packed[:, index] for index in range(HALVES)], axis=-1)
+        return wide.reshape(count * part, width)
 
     def remote(source, target, send, recv, where):
         return pltpu.make_async_remote_copy(
@@ -217,7 +225,7 @@
     load_o = pltpu.make_async_copy(w_out, wo, local_sem.at[1])
     load_p = pltpu.make_async_copy(w_pair, wp, local_sem.at[2])
     load_own = pltpu.make_async_copy(
-        frames.at[at(s * cols)], tokens.at[slab(u, s, h)], local_sem.at[3]
+        frames, own_frames, local_sem.at[3]
     )
     small = [
         pltpu.make_async_copy(source, target, local_sem.at[5 + index])
@@ -237,6 +245,18 @@
     load_o.start()
     load_p.start()
 
+    load_own.wait()
+    for t in range(S):
+        for half in range(HALVES):
+            start = t * cols
+            slab = own_frames[start : start + cols, :].astype(jnp.float32)
+            slab = slab[half * part : (half + 1) * part]
+            span = width // HALVES
+            packed = [slab[:, k * span : (k + 1) * span] for k in range(HALVES)]
+            outgoing[half, t] = jnp.concatenate(packed, axis=0).astype(jnp.bfloat16)
+    for half in range(HALVES):
+        tokens[half, order(u, s, h)] = outgoing[half, s]
+
     barrier = pltpu.get_barrier_semaphore()
 
     def greet(step, carry):
@@ -252,100 +272,97 @@
 
     steps = sorted(range(S), key=lambda d: min(d, S - d))
 
-    for dz in reversed(steps[1:]):
-        t = lax.rem(s + dz, S)
-        send(
-            frames.at[at(t * cols)],
-            tokens.at[slab(u, s, h)],
-            a_send.at[dz - 1],
-            a_recv.at[dz - 1],
-            {"seq": t},
-        )
-
-    def to_heads(dz):
-        s_ = lax.rem(s + S - dz, S)
-        place = tokens.at[slab(u, s_, h)]
+    def to_seq(half):
+        for dz in reversed(steps[1:]):
+            t = lax.rem(s + dz, S)
+            send(
+                outgoing.at[half, t],
+                tokens.at[half, order(u, s, h)],
+                a_send.at[half, dz - 1],
+                a_recv.at[half, dz - 1],
+                {"seq": t},
+            )
+
+    def to_heads(half, dz):
+        place = tokens.at[half, order(u, behind(dz), h)]
+        if dz:
+            remote(
+                place, place, a_send.at[half, dz - 1], a_recv.at[half, dz - 1], {"seq": s}
+            ).wait_recv()
         for dh in range(1, H):
             send(
                 place,
                 place,
-                b_send.at[dh - 1, dz],
-                b_recv.at[dh - 1, dz],
+                b_send.at[half, dh - 1, dz],
+                b_recv.at[half, dh - 1, dz],
                 {"head": lax.rem(h + dh, H)},
             )
-        to_subs(0, dz)
-
-    def to_subs(dh, dz):
-        place = tokens.at[slab(u, lax.rem(s + S - dz, S), lax.rem(h + H - dh, H))]
+
+    def to_subs(half, dz):
+        s_ = behind(dz)
+        for dh in range(1, H):
+            place = tokens.at[half, order(u, s_, lax.rem(h + H - dh, H))]
+            remote(
+                place, place, b_send.at[half, dh - 1, dz], b_recv.at[half, dh - 1, dz], {"head": h}
+            ).wait_recv()
+        place = tokens.at[half, pl.ds(order(u, s_, 0), H)]
         for du in range(1, U):
             send(
                 place,
                 place,
-                c_send.at[du - 1, dh, dz],
-                c_recv.at[du - 1, dh, dz],
+                c_send.at[half, du - 1, dz],
+                c_recv.at[half, du - 1, dz],
                 {"sub": lax.rem(u + du, U)},
             )
-
-    def from_heads(dz):
-        s_ = lax.rem(s + S - dz, S)
-        for dh in range(1, H):
-            place = tokens.at[slab(u, s_, lax.rem(h + H - dh, H))]
-            remote(
-                place, place, b_send.at[dh - 1, dz], b_recv.at[dh - 1, dz], {"head": h}
-            ).wait_recv()
-            to_subs(dh, dz)
 
     def scale(values, gain):
         floats = values.astype(jnp.float32)
         mean_sq = jnp.mean(floats * floats, axis=-1, keepdims=True)
         return floats * lax.rsqrt(mean_sq + 1e-06) * gain[...][None, :]
 
-    def normalize_piece(u_, s_):
-        place = at((u_ * S + s_) * chunk, chunk)
-        scaled = scale(tokens[place, :], attn_gain)
-        for half in range(HALVES):
-            target = at(half * half_rows + (u_ * S + s_) * H * part, H * part)
-            normed[target, :] = halved(scaled, half).astype(jnp.bfloat16)
-
-    load_own.wait()
-    to_heads(0)
-    for load in small:
-        load.wait()
-    for index, dz in enumerate(steps):
-        if index + 1 < S:
-            ahead = steps[index + 1]
-            place = tokens.at[slab(u, lax.rem(s + S - ahead, S), h)]
-            remote(
-                place, place, a_send.at[ahead - 1], a_recv.at[ahead - 1], {"seq": s}
-            ).wait_recv()
-            to_heads(ahead)
-        from_heads(dz)
-        normalize_piece(u, lax.rem(s + S - dz, S))
-    for dz in steps:
-        s_ = lax.rem(s + S - dz, S)
-        for du in range(1, U):
-            u_ = lax.rem(u + U - du, U)
-            for dh in range(H):
-                place = tokens.at[slab(u_, s_, lax.rem(h + H - dh, H))]
+    def normalize_piece(half, u_, s_):
+        scaled = scale(unpack(half, order(u_, s_, 0), H), attn_gain)
+        target = at(half * half_rows + (u_ * S + s_) * H * part, H * part)
+        normed[target, :] = scaled.astype(jnp.bfloat16)
+
+    def normalize_half(half):
+        for dz in steps:
+            normalize_piece(half, u, behind(dz))
+        for dz in steps:
+            s_ = behind(dz)
+            for du in range(1, U):
+                u_ = lax.rem(u + U - du, U)
+                place = tokens.at[half, pl.ds(order(u_, s_, 0), H)]
                 remote(
                     place,
                     place,
-                    c_send.at[du - 1, dh, dz],
-                    c_recv.at[du - 1, dh, dz],
+                    c_send.at[half, du - 1, dz],
+                    c_recv.at[half, du - 1, dz],
                     {"sub": u},
                 ).wait_recv()
-            normalize_piece(u_, s_)
-
+                normalize_piece(half, u_, s_)
+
+    to_seq(0)
+    to_heads(0, 0)
+    for half in range(1, HALVES):
+        to_seq(half)
+    for load in small:
+        load.wait()
+    for dz in steps[1:]:
+        to_heads(0, dz)
+    for dz in steps:
+        to_subs(0, dz)
+        for half in range(1, HALVES):
+            to_heads(half, dz)
+    normalize_half(0)
     load_q.wait()
     first = lax.broadcasted_iota(jnp.int32, (half_rows, half_rows), 0)
     second = lax.broadcasted_iota(jnp.int32, (half_rows, half_rows), 1)
     together = lax.rem(first, part) == lax.rem(second, part)
 
-    def project(head):
-        base = head * 3 * head_dim
-        qkv[base : base + 3 * head_dim, :] = nt_dot(
-            wq[base : base + 3 * head_dim, :], normed[...]
-        ).astype(jnp.bfloat16)
+    def project(half):
+        lanes = slice(half * half_rows, (half + 1) * half_rows)
+        qkv[:, lanes] = nt_dot(wq[...], normed[lanes, :]).astype(jnp.bfloat16)
 
     def attend(head, half):
         base = head * 3 * head_dim
@@ -399,19 +416,19 @@
                     {"head": lax.rem(h + dh, H)},
                 )
 
-    for head in range(heads):
-        project(head)
-        attend(head, 0)
-    load_o.wait()
-    output(0)
-    for half in range(1, HALVES):
-        for head in range(heads // 2):
+    for half in range(HALVES):
+        project(half)
+        if half + 1 < HALVES:
+            for dz in steps:
+                to_subs(half + 1, dz)
+        for head in range(heads):
             attend(head, half)
-        exchange(half - 1)
-        for head in range(heads // 2, heads):
-            attend(head, half)
+        if half == 0:
+            load_o.wait()
         output(half)
-    exchange(HALVES - 1)
+        if half + 1 < HALVES:
+            normalize_half(half + 1)
+        exchange(half)
 
     def finish(p):
         half, index = divmod(p, PIECES)
@@ -423,9 +440,7 @@
                 landed, landed, e_send.at[dh - 1, p], e_recv.at[dh - 1, p], {"head": h}
             ).wait_recv()
             value = value + head_recv[dh - 1, place, :].astype(jnp.float32)
-        block = piece_rows * HALVES
-        source = at(u * unit + index * block, block)
-        value = value + halved(tokens[source, :].astype(jnp.float32), half)
+        value = value + unpack(half, order(u, index * piece_seq, 0), piece_seq * H)
         value = value.astype(jnp.bfloat16)
         wide = value.astype(jnp.float32)
         hidden_wide[half, index * piece_seq : (index + 1) * piece_seq] = wide.reshape(
@@ -528,8 +543,8 @@
             place, place, q_send.at[step - 1], q_recv.at[step - 1], {"seq": s}
         ).wait_recv()
 
-    order = lax.broadcasted_iota(jnp.int32, (N, picks), 0)
-    frame = lax.rem(order, S * H) * U + order // (S * H)
+    row = lax.broadcasted_iota(jnp.int32, (N, picks), 0)
+    frame = lax.rem(row, S * H) * U + row // (S * H)
     share = N // rolls
     for roll in range(rolls):
         total = scored[roll * share, :actions_n, :N]
@@ -578,7 +593,9 @@
             pltpu.VMEM((width,), f32),
             pltpu.VMEM((actions_n, out_width), f32),
             pltpu.VMEM((rolls, picks), jnp.int32),
-            pltpu.VMEM((rows, width), bf16),
+            pltpu.VMEM((rows_own, width), bf16),
+            pltpu.VMEM((HALVES, S, cols, width // HALVES), bf16),
+            pltpu.VMEM((HALVES, N, cols, width // HALVES), bf16),
             pltpu.VMEM((rows, width), bf16),
             pltpu.VMEM((heads * 3 * head_dim, width), bf16),
             pltpu.VMEM(w_out.shape, bf16),
@@ -596,12 +613,12 @@
             pltpu.VMEM((rows, width), bf16),
             pltpu.VMEM((N, -(-actions_n // 8) * 8, -(-N // 128) * 128), f32),
             dma((9,)),
-            dma((S - 1,)),
-            dma((S - 1,)),
-            dma((H - 1, S)),
-            dma((H - 1, S)),
-            dma((U - 1, H, S)),
-            dma((U - 1, H, S)),
+            dma((HALVES, S - 1)),
+            dma((HALVES, S - 1)),
+            dma((HALVES, H - 1, S)),
+            dma((HALVES, H - 1, S)),
+            dma((HALVES, U - 1, S)),
+            dma((HALVES, U - 1, S)),
             dma((U - 1, HALVES * PIECES)),
             dma((U - 1, HALVES * PIECES)),
             dma((H - 1, HALVES * PIECES)),

time: 45.8 us -> 43.5 us (0.950)
  Pallas kernels: 42.1 us -> 39.7 us
    pallas_call x1, Pallas kernels: 42.1 us -> 39.7 us  [shards(): pl.pallas_call(functools.partial(fused_kernel, (S, H, U, heads, head_dim)...]
where the time goes in v4:
time: 43.5 us; the launch traced here: 43.3 us
  Pallas kernels  39.7 us (91%)
  local copies, waits for them, and re-layouts  2.9 us (7%)
  between operations  0.64 us (1%)
    pallas_call x1, Pallas kernels, shards(): pl.pallas_call(functools.partial(fused_kernel, (S, H, U, heads, head_dim)...  39.7 us
    unnamed x2, local copies, waits for them, and re-layouts  2.9 us

profile of v4, /device:TPU:0, one launch (start us, length us, event | category | flops | bytes accessed | tf_op | source)
XLA Modules:
  0.0 43.3 jit_solution(4812545677458394866)
XLA Ops:
  0.6 39.7 %shard_map.95 = (bf16[64,1536]{1,0:T(8,128)(2,1)}, f32[7,2,15]{2,1,0:T(2,128)}) custom-call(bf16[64,1536]{1,0:T(8,128)(2,1)} %frames.1, f32[1536]{0:T(1024)} %attn_gain_in.1, bf16[1152,1536]{1,0:T(8,128)(2,1)} %bitcast.5, bf16[384,1536]{1,0:T(8,128)(2,1)} %w_out.1, f32[1536]{0:T(1024)} %vit_gain_in.1, bf16[2,1536,256]{2,1,0:T(8,128)(2,1)} %w_pair.1, ...), custom_call_target="tpu_custom_call" | custom-call | tf_op jit(solution)/shard_map/pallas_call | solution.py:583
  40.4 1.6 %copy.12 = bf16[64,1536]{1,0:T(8,128)(2,1)} copy(bf16[64,1536]{1,0:T(8,128)(2,1)} %get-tuple-element.8) | data formatting | bytes 393216
  42.0 1.3 %copy.13 = f32[2,15,7]{1,0,2:T(2,128)} copy(f32[2,15,7]{1,0,2:T(2,128)} %bitcast.7) | data formatting | bytes 1680

commit v5 on v4

--- a/solution.py
+++ b/solution.py
@@ -364,17 +364,23 @@
         lanes = slice(half * half_rows, (half + 1) * half_rows)
         qkv[:, lanes] = nt_dot(wq[...], normed[lanes, :]).astype(jnp.bfloat16)
 
-    def attend(head, half):
-        base = head * 3 * head_dim
+    def attend(half):
         lanes = slice(half * half_rows, (half + 1) * half_rows)
-        queries = qkv[base : base + head_dim, lanes]
-        keys = qkv[base + head_dim : base + 2 * head_dim, lanes]
-        values = qkv[base + 2 * head_dim : base + 3 * head_dim, lanes]
-        scores = jnp.where(together, tn_dot(keys, queries) * head_dim ** (-0.5), -1e30)
-        weights = jnp.exp(scores - jnp.max(scores, axis=0, keepdims=True))
-        total = jnp.sum(weights, axis=0, keepdims=True)
-        out = jnp.dot(values, weights.astype(jnp.bfloat16), preferred_element_type=jnp.float32)
-        mixed[head * head_dim : (head + 1) * head_dim, lanes] = (out / total).astype(jnp.bfloat16)
+
+        def cut(head, index):
+            base = (head * 3 + index) * head_dim
+            return qkv[base : base + head_dim, lanes]
+
+        scores = jnp.stack([tn_dot(cut(head, 1), cut(head, 0)) for head in range(heads)])
+        scores = jnp.where(together[None], scores * head_dim ** (-0.5), -1e30)
+        weights = jnp.exp(scores - jnp.max(scores, axis=1, keepdims=True))
+        total = 1.0 / jnp.sum(weights, axis=1, keepdims=True)
+        weights = (weights * total).astype(jnp.bfloat16)
+        outs = [
+            jnp.dot(cut(head, 2), weights[head], preferred_element_type=jnp.float32)
+            for head in range(heads)
+        ]
+        mixed[:, lanes] = jnp.concatenate(outs, axis=0).astype(jnp.bfloat16)
 
     def output(half):
         lanes = slice(half * half_rows, (half + 1) * half_rows)
@@ -421,8 +427,7 @@
         if half + 1 < HALVES:
             for dz in steps:
                 to_subs(half + 1, dz)
-        for head in range(heads):
-            attend(head, half)
+        attend(half)
         if half == 0:
             load_o.wait()
         output(half)
@@ -557,6 +562,17 @@
 
     for copy in sent:
         copy.wait_send()
+
+
+def write_kernel(hidden_in, actions_in, hidden_out, actions_out, sem):
+    copies = [
+        pltpu.make_async_copy(hidden_in, hidden_out, sem.at[0]),
+        pltpu.make_async_copy(actions_in, actions_out, sem.at[1]),
+    ]
+    for copy in copies:
+        copy.start()
+    for copy in copies:
+        copy.wait()
 
 
 def shards(frames_in, attn_gain, w_qkv, w_out, vit_gain, w_pair, w_act, pair_frames):
@@ -643,6 +659,17 @@
         jnp.transpose(w_act, (1, 0)),
         pair_frames,
     )
+    hidden, actions = pl.pallas_call(
+        write_kernel,
+        out_shape=(
+            jax.ShapeDtypeStruct(hidden.shape, bf16),
+            jax.ShapeDtypeStruct(actions.shape, f32),
+        ),
+        in_specs=[anywhere] * 2,
+        out_specs=(anywhere, anywhere),
+        scratch_shapes=[dma((2,))],
+        compiler_params=pltpu.CompilerParams(vmem_limit_bytes=60 * 1024 * 1024),
+    )(hidden, actions)
     return (hidden, jnp.transpose(actions, (1, 2, 0)))
 
 

time: 43.5 us -> 46.5 us (1.069)
  Pallas kernels: 39.7 us -> 45.8 us
  local copies, waits for them, and re-layouts: 2.9 us -> 0 us
    pallas_call x0 -> x1, Pallas kernels: none -> 7.29 us  [shards(): pl.pallas_call(write_kernel, out_shape=(jax.ShapeDtypeStruct(hidden.shape...]
    unnamed x2 -> x0, local copies, waits for them, and re-layouts: 2.9 us -> none
    pallas_call x1, Pallas kernels: 39.7 us -> 38.5 us  [shards(): pl.pallas_call(functools.partial(fused_kernel, (S, H, U, heads, head_dim)...]
where the time goes in v5:
time: 46.5 us; the launch traced here: 46.4 us
  Pallas kernels  45.8 us (98%)
  between operations  0.64 us (1%)
    pallas_call x1, Pallas kernels, shards(): pl.pallas_call(functools.partial(fused_kernel, (S, H, U, heads, head_dim)...  38.5 us
    pallas_call x1, Pallas kernels, shards(): pl.pallas_call(write_kernel, out_shape=(jax.ShapeDtypeStruct(hidden.shape...  7.29 us

profile of v5, /device:TPU:0, one launch (start us, length us, event | category | flops | bytes accessed | tf_op | source)
XLA Modules:
  0.0 46.4 jit_solution(13644016161006190745)
XLA Ops:
  0.6 38.5 %shard_map.95 = (bf16[64,1536]{1,0:T(8,128)(2,1)}, f32[7,2,15]{2,1,0:T(2,128)}) custom-call(bf16[64,1536]{1,0:T(8,128)(2,1)} %frames.1, f32[1536]{0:T(1024)} %attn_gain_in.1, bf16[1152,1536]{1,0:T(8,128)(2,1)} %bitcast.5, bf16[384,1536]{1,0:T(8,128)(2,1)} %w_out.1, f32[1536]{0:T(1024)} %vit_gain_in.1, bf16[2,1536,256]{2,1,0:T(8,128)(2,1)} %w_pair.1, ...), custom_call_target="tpu_custom_call" | custom-call | tf_op jit(solution)/shard_map/pallas_call | solution.py:599
  39.1 7.3 %shard_map.96 = (bf16[64,1536]{1,0:T(8,128)(2,1)}, f32[7,2,15]{2,1,0:T(2,128)}) custom-call(bf16[64,1536]{1,0:T(8,128)(2,1)} %get-tuple-element.6.hidden_in, f32[7,2,15]{2,1,0:T(2,128)} %get-tuple-element.7.actions_in), custom_call_target="tpu_custom_call" | custom-call | tf_op jit(solution)/shard_map/pallas_call | solution.py:662

commit v6 on v5

--- a/solution.py
+++ b/solution.py
@@ -245,6 +245,17 @@
     load_o.start()
     load_p.start()
 
+    barrier = pltpu.get_barrier_semaphore()
+
+    def greet(step, carry):
+        other = lax.rem(me + step, N)
+        where = {"seq": other // (H * U), "head": other // U % H, "sub": other % U}
+        pl.semaphore_signal(
+            barrier, inc=1, device_id=where, device_id_type=pl.DeviceIdType.MESH
+        )
+        return carry
+
+    lax.fori_loop(1, N, greet, 0)
     load_own.wait()
     for t in range(S):
         for half in range(HALVES):
@@ -257,17 +268,6 @@
     for half in range(HALVES):
         tokens[half, order(u, s, h)] = outgoing[half, s]
 
-    barrier = pltpu.get_barrier_semaphore()
-
-    def greet(step, carry):
-        other = lax.rem(me + step, N)
-        where = {"seq": other // (H * U), "head": other // U % H, "sub": other % U}
-        pl.semaphore_signal(
-            barrier, inc=1, device_id=where, device_id_type=pl.DeviceIdType.MESH
-        )
-        return carry
-
-    lax.fori_loop(1, N, greet, 0)
     pl.semaphore_wait(barrier, N - 1)
 
     steps = sorted(range(S), key=lambda d: min(d, S - d))
@@ -344,16 +344,15 @@
 
     to_seq(0)
     to_heads(0, 0)
-    for half in range(1, HALVES):
-        to_seq(half)
     for load in small:
         load.wait()
     for dz in steps[1:]:
         to_heads(0, dz)
+    for half in range(1, HALVES):
+        to_seq(half)
+        to_heads(half, 0)
     for dz in steps:
         to_subs(0, dz)
-        for half in range(1, HALVES):
-            to_heads(half, dz)
     normalize_half(0)
     load_q.wait()
     first = lax.broadcasted_iota(jnp.int32, (half_rows, half_rows), 0)
@@ -423,17 +422,21 @@
                 )
 
     for half in range(HALVES):
+        following = steps[1:] if half + 1 < HALVES else []
         project(half)
+        for dz in following[:1]:
+            to_heads(half + 1, dz)
+        attend(half)
+        for dz in following[1:]:
+            to_heads(half + 1, dz)
+        if half == 0:
+            load_o.wait()
+        output(half)
+        exchange(half)
         if half + 1 < HALVES:
             for dz in steps:
                 to_subs(half + 1, dz)
-        attend(half)
-        if half == 0:
-            load_o.wait()
-        output(half)
-        if half + 1 < HALVES:
             normalize_half(half + 1)
-        exchange(half)
 
     def finish(p):
         half, index = divmod(p, PIECES)
@@ -564,15 +567,9 @@
         copy.wait_send()
 
 
-def write_kernel(hidden_in, actions_in, hidden_out, actions_out, sem):
-    copies = [
-        pltpu.make_async_copy(hidden_in, hidden_out, sem.at[0]),
-        pltpu.make_async_copy(actions_in, actions_out, sem.at[1]),
-    ]
-    for copy in copies:
-        copy.start()
-    for copy in copies:
-        copy.wait()
+def write_kernel(hidden_in, actions_in, hidden_out, actions_out):
+    hidden_out[...] = hidden_in[...]
+    actions_out[...] = actions_in[...]
 
 
 def shards(frames_in, attn_gain, w_qkv, w_out, vit_gain, w_pair, w_act, pair_frames):
@@ -665,10 +662,8 @@
             jax.ShapeDtypeStruct(hidden.shape, bf16),
             jax.ShapeDtypeStruct(actions.shape, f32),
         ),
-        in_specs=[anywhere] * 2,
-        out_specs=(anywhere, anywhere),
-        scratch_shapes=[dma((2,))],
-        compiler_params=pltpu.CompilerParams(vmem_limit_bytes=60 * 1024 * 1024),
+        in_specs=[vmem] * 2,
+        out_specs=(vmem, vmem),
     )(hidden, actions)
     return (hidden, jnp.transpose(actions, (1, 2, 0)))
 

time: 46.5 us -> 41.1 us (0.88)
  Pallas kernels: 45.8 us -> 40.3 us
    pallas_call x1, Pallas kernels: 7.29 us -> 1.62 us  [shards(): pl.pallas_call(write_kernel, out_shape=(jax.ShapeDtypeStruct(hidden.shape...]
where the time goes in v6:
time: 41.1 us; the launch traced here: 40.9 us
  Pallas kernels  40.3 us (98%)
  between operations  0.64 us (2%)
    pallas_call x1, Pallas kernels, shards(): pl.pallas_call(functools.partial(fused_kernel, (S, H, U, heads, head_dim)...  38.7 us
    pallas_call x1, Pallas kernels, shards(): pl.pallas_call(write_kernel, out_shape=(jax.ShapeDtypeStruct(hidden.shape...  1.62 us

profile of v6, /device:TPU:0, one launch (start us, length us, event | category | flops | bytes accessed | tf_op | source)
XLA Modules:
  0.0 40.9 jit_solution(6817278584354533804)
XLA Ops:
  0.6 38.7 %shard_map.95 = (bf16[64,1536]{1,0:T(8,128)(2,1)}, f32[7,2,15]{2,1,0:T(2,128)}) custom-call(bf16[64,1536]{1,0:T(8,128)(2,1)} %frames.1, f32[1536]{0:T(1024)} %attn_gain_in.1, bf16[1152,1536]{1,0:T(8,128)(2,1)} %bitcast.5, bf16[384,1536]{1,0:T(8,128)(2,1)} %w_out.1, f32[1536]{0:T(1024)} %vit_gain_in.1, bf16[2,1536,256]{2,1,0:T(8,128)(2,1)} %w_pair.1, ...), custom_call_target="tpu_custom_call" | custom-call | tf_op jit(solution)/shard_map/pallas_call | solution.py:596
  39.3 1.6 %shard_map.96 = (bf16[64,1536]{1,0:T(8,128)(2,1)}, f32[7,2,15]{2,1,0:T(2,128)}) custom-call(bf16[64,1536]{1,0:T(8,128)(2,1)} %get-tuple-element.6.hidden_in, f32[7,2,15]{2,1,0:T(2,128)} %get-tuple-element.7.actions_in), custom_call_target="tpu_custom_call" | custom-call | tf_op jit(solution)/shard_map/pallas_call | solution.py:659

commit v7 on v6

--- a/solution.py
+++ b/solution.py
@@ -145,6 +145,7 @@
     hidden_wide,
     hidden,
     vit,
+    grouped,
     scored,
     local_sem,
     a_send,
@@ -161,6 +162,8 @@
     v_recv,
     o_send,
     o_recv,
+    p_send,
+    p_recv,
     q_send,
     q_recv,
 ):
@@ -179,7 +182,6 @@
     actions_n, rolls, picks = actions_out.shape
     out_width = wp.shape[2]
     s, h, u = lax.axis_index("seq"), lax.axis_index("head"), lax.axis_index("sub")
-    me = (s * H + h) * U + u
 
     def at(value, size=cols):
         return pl.ds(pl.multiple_of(value, size), size)
@@ -247,15 +249,21 @@
 
     barrier = pltpu.get_barrier_semaphore()
 
-    def greet(step, carry):
-        other = lax.rem(me + step, N)
-        where = {"seq": other // (H * U), "head": other // U % H, "sub": other % U}
+    G = H * U
+    mine = h * U + u
+
+    def group_peer(step):
+        other = lax.rem(mine + step, G)
+        return {"head": other // U, "sub": lax.rem(other, U)}
+
+    def seq_peer(step):
+        return {"seq": lax.rem(s + step, S)}
+
+    peers = [group_peer(step) for step in range(1, G)] + [seq_peer(step) for step in range(1, S)]
+    for where in peers:
         pl.semaphore_signal(
             barrier, inc=1, device_id=where, device_id_type=pl.DeviceIdType.MESH
         )
-        return carry
-
-    lax.fori_loop(1, N, greet, 0)
     load_own.wait()
     for t in range(S):
         for half in range(HALVES):
@@ -268,7 +276,7 @@
     for half in range(HALVES):
         tokens[half, order(u, s, h)] = outgoing[half, s]
 
-    pl.semaphore_wait(barrier, N - 1)
+    pl.semaphore_wait(barrier, len(peers))
 
     steps = sorted(range(S), key=lambda d: min(d, S - d))
 
@@ -432,7 +440,14 @@
         if half == 0:
             load_o.wait()
         output(half)
+        early = sent[:]
+        sent.clear()
         exchange(half)
+        if half + 1 == HALVES:
+            for copy in early:
+                copy.wait_send()
+        else:
+            sent.extend(early)
         if half + 1 < HALVES:
             for dz in steps:
                 to_subs(half + 1, dz)
@@ -454,12 +469,12 @@
         hidden_wide[half, index * piece_seq : (index + 1) * piece_seq] = wide.reshape(
             piece_seq, H, part, width
         )
-        mine = vit_piece(u, p)
-        vit[mine, :] = scale(value, vit_gain).astype(jnp.bfloat16)
+        placed = vit_piece(u, p)
+        vit[placed, :] = scale(value, vit_gain).astype(jnp.bfloat16)
         for du in range(1, U):
             send(
-                vit.at[mine],
-                vit.at[mine],
+                vit.at[placed],
+                vit.at[placed],
                 v_send.at[du - 1, p],
                 v_recv.at[du - 1, p],
                 {"sub": lax.rem(u + du, U)},
@@ -516,13 +531,19 @@
                     send_hidden(s_)
         pooled = pooled + embed(half)
     pooled = pooled * (rolls / (cols * S))
-    scored[me, :actions_n, :N] = nt_dot(w_act[...], pooled, precision=lax.Precision.HIGHEST)
-
-    for step in range(1, N):
-        other = lax.rem(me + step, N)
-        where = {"seq": other // (H * U), "head": other // U % H, "sub": other % U}
-        send(scored.at[me], scored.at[me], q_send.at[step - 1], q_recv.at[step - 1], where)
-
+    grouped[mine, :actions_n, :N] = nt_dot(w_act[...], pooled, precision=lax.Precision.HIGHEST)
+    early = sent[:]
+    sent.clear()
+    for step in range(1, G):
+        send(
+            grouped.at[mine],
+            grouped.at[mine],
+            p_send.at[step - 1],
+            p_recv.at[step - 1],
+            group_peer(step),
+        )
+    for copy in early:
+        copy.wait_send()
     for dz in range(1, S):
         s_ = lax.rem(s + dz, S)
         remote(
@@ -532,28 +553,44 @@
             o_recv.at[dz - 1],
             {"seq": s},
         ).wait_send()
-        from_ = lax.rem(s + S - dz, S)
+    for step in range(1, G):
+        place = grouped.at[lax.rem(mine + G - step, G)]
         remote(
-            hidden.at[s_],
+            place, place, p_send.at[step - 1], p_recv.at[step - 1], {"seq": s}
+        ).wait_recv()
+    total = grouped[0, :actions_n, :N]
+    for index in range(1, G):
+        total = total + grouped[index, :actions_n, :N]
+    scored[s, :actions_n, :N] = total
+    for step in range(1, S):
+        send(
+            scored.at[s],
+            scored.at[s],
+            q_send.at[step - 1],
+            q_recv.at[step - 1],
+            seq_peer(step),
+        )
+    for dz in range(1, S):
+        from_ = behind(dz)
+        remote(
+            hidden.at[from_],
             hidden_out.at[at(from_ * cols)],
             o_send.at[dz - 1],
             o_recv.at[dz - 1],
             {"seq": s},
         ).wait_recv()
-    pltpu.make_async_copy(
-        hidden.at[s], hidden_out.at[at(s * cols)], local_sem.at[4]
-    ).wait()
-
-    for step in range(1, N):
-        other = lax.rem(me + N - step, N)
-        place = scored.at[other]
+    pltpu.make_async_copy(hidden.at[s], hidden_out.at[at(s * cols)], local_sem.at[4]).wait()
+    for copy in sent:
+        copy.wait_send()
+    for step in range(1, S):
+        place = scored.at[behind(step)]
         remote(
             place, place, q_send.at[step - 1], q_recv.at[step - 1], {"seq": s}
         ).wait_recv()
 
     row = lax.broadcasted_iota(jnp.int32, (N, picks), 0)
     frame = lax.rem(row, S * H) * U + row // (S * H)
-    share = N // rolls
+    share = S // rolls
     for roll in range(rolls):
         total = scored[roll * share, :actions_n, :N]
         for index in range(1, share):
@@ -562,10 +599,6 @@
         actions_out[:, roll, :] = jnp.dot(
             total, chosen, preferred_element_type=jnp.float32, precision=lax.Precision.HIGHEST
         )
-
-    for copy in sent:
-        copy.wait_send()
-
 
 def write_kernel(hidden_in, actions_in, hidden_out, actions_out):
     hidden_out[...] = hidden_in[...]
@@ -624,7 +657,8 @@
             pltpu.VMEM((HALVES, S, H, cols // HALVES, width), f32),
             pltpu.VMEM((S, cols, width), bf16),
             pltpu.VMEM((rows, width), bf16),
-            pltpu.VMEM((N, -(-actions_n // 8) * 8, -(-N // 128) * 128), f32),
+            pltpu.VMEM((H * U, -(-actions_n // 8) * 8, -(-N // 128) * 128), f32),
+            pltpu.VMEM((S, -(-actions_n // 8) * 8, -(-N // 128) * 128), f32),
             dma((9,)),
             dma((HALVES, S - 1)),
             dma((HALVES, S - 1)),
@@ -640,8 +674,10 @@
             dma((U - 1, HALVES * PIECES)),
             dma((S - 1,)),
             dma((S - 1,)),
-            dma((N - 1,)),
-            dma((N - 1,)),
+            dma((H * U - 1,)),
+            dma((H * U - 1,)),
+            dma((S - 1,)),
+            dma((S - 1,)),
         ],
         compiler_params=pltpu.CompilerParams(
             collective_id=0, has_side_effects=True, vmem_limit_bytes=60 * 1024 * 1024

time: 41.1 us -> 41.7 us (1.015)
  Pallas kernels: 40.3 us -> 40.9 us
    pallas_call x1, Pallas kernels: 38.7 us -> 39.3 us  [shards(): pl.pallas_call(functools.partial(fused_kernel, (S, H, U, heads, head_dim)...]
where the time goes in v7:
time: 41.7 us; the launch traced here: 41.6 us
  Pallas kernels  40.9 us (98%)
  between operations  0.64 us (2%)
    pallas_call x1, Pallas kernels, shards(): pl.pallas_call(functools.partial(fused_kernel, (S, H, U, heads, head_dim)...  39.3 us
    pallas_call x1, Pallas kernels, shards(): pl.pallas_call(write_kernel, out_shape=(jax.ShapeDtypeStruct(hidden.shape...  1.62 us

profile of v7, /device:TPU:0, one launch (start us, length us, event | category | flops | bytes accessed | tf_op | source)
XLA Modules:
  0.0 41.6 jit_solution(13103269212717332483)
XLA Ops:
  0.6 39.3 %shard_map.95 = (bf16[64,1536]{1,0:T(8,128)(2,1)}, f32[7,2,15]{2,1,0:T(2,128)}) custom-call(bf16[64,1536]{1,0:T(8,128)(2,1)} %frames.1, f32[1536]{0:T(1024)} %attn_gain_in.1, bf16[1152,1536]{1,0:T(8,128)(2,1)} %bitcast.5, bf16[384,1536]{1,0:T(8,128)(2,1)} %w_out.1, f32[1536]{0:T(1024)} %vit_gain_in.1, bf16[2,1536,256]{2,1,0:T(8,128)(2,1)} %w_pair.1, ...), custom_call_target="tpu_custom_call" | custom-call | tf_op jit(solution)/shard_map/pallas_call | solution.py:629
  40.0 1.6 %shard_map.96 = (bf16[64,1536]{1,0:T(8,128)(2,1)}, f32[7,2,15]{2,1,0:T(2,128)}) custom-call(bf16[64,1536]{1,0:T(8,128)(2,1)} %get-tuple-element.6.hidden_in, f32[7,2,15]{2,1,0:T(2,128)} %get-tuple-element.7.actions_in), custom_call_target="tpu_custom_call" | custom-call | tf_op jit(solution)/shard_map/pallas_call | solution.py:695

commit v8 on v6

--- a/solution.py
+++ b/solution.py
@@ -342,15 +342,13 @@
                 ).wait_recv()
                 normalize_piece(half, u_, s_)
 
-    to_seq(0)
-    to_heads(0, 0)
+    for half in range(HALVES):
+        to_seq(half)
+        to_heads(half, 0)
     for load in small:
         load.wait()
     for dz in steps[1:]:
         to_heads(0, dz)
-    for half in range(1, HALVES):
-        to_seq(half)
-        to_heads(half, 0)
     for dz in steps:
         to_subs(0, dz)
     normalize_half(0)
@@ -422,21 +420,29 @@
                 )
 
     for half in range(HALVES):
-        following = steps[1:] if half + 1 < HALVES else []
+        later = half + 1 < HALVES
+        following = steps[1:] if later else []
+        for dz in following[:2]:
+            to_heads(half + 1, dz)
         project(half)
-        for dz in following[:1]:
+        for dz in following[2:]:
             to_heads(half + 1, dz)
         attend(half)
-        for dz in following[1:]:
-            to_heads(half + 1, dz)
         if half == 0:
             load_o.wait()
         output(half)
-        exchange(half)
-        if half + 1 < HALVES:
+        if later:
             for dz in steps:
                 to_subs(half + 1, dz)
+        early = sent[:]
+        sent.clear()
+        exchange(half)
+        if later:
+            sent.extend(early)
             normalize_half(half + 1)
+        else:
+            for copy in early:
+                copy.wait_send()
 
     def finish(p):
         half, index = divmod(p, PIECES)
@@ -518,11 +524,15 @@
     pooled = pooled * (rolls / (cols * S))
     scored[me, :actions_n, :N] = nt_dot(w_act[...], pooled, precision=lax.Precision.HIGHEST)
 
+    early = sent[:]
+    sent.clear()
     for step in range(1, N):
         other = lax.rem(me + step, N)
         where = {"seq": other // (H * U), "head": other // U % H, "sub": other % U}
         send(scored.at[me], scored.at[me], q_send.at[step - 1], q_recv.at[step - 1], where)
 
+    for copy in early:
+        copy.wait_send()
     for dz in range(1, S):
         s_ = lax.rem(s + dz, S)
         remote(

time: 41.1 us -> 40.6 us (0.988)
    pallas_call x1, Pallas kernels: 38.7 us -> 38.2 us  [shards(): pl.pallas_call(functools.partial(fused_kernel, (S, H, U, heads, head_dim)...]
where the time goes in v8:
time: 40.6 us; the launch traced here: 40.5 us
  Pallas kernels  39.9 us (98%)
  between operations  0.64 us (2%)
    pallas_call x1, Pallas kernels, shards(): pl.pallas_call(functools.partial(fused_kernel, (S, H, U, heads, head_dim)...  38.2 us
    pallas_call x1, Pallas kernels, shards(): pl.pallas_call(write_kernel, out_shape=(jax.ShapeDtypeStruct(hidden.shape...  1.62 us

profile of v8, /device:TPU:0, one launch (start us, length us, event | category | flops | bytes accessed | tf_op | source)
XLA Modules:
  0.0 40.5 jit_solution(11156618111694524222)
XLA Ops:
  0.6 38.2 %shard_map.95 = (bf16[64,1536]{1,0:T(8,128)(2,1)}, f32[7,2,15]{2,1,0:T(2,128)}) custom-call(bf16[64,1536]{1,0:T(8,128)(2,1)} %frames.1, f32[1536]{0:T(1024)} %attn_gain_in.1, bf16[1152,1536]{1,0:T(8,128)(2,1)} %bitcast.5, bf16[384,1536]{1,0:T(8,128)(2,1)} %w_out.1, f32[1536]{0:T(1024)} %vit_gain_in.1, bf16[2,1536,256]{2,1,0:T(8,128)(2,1)} %w_pair.1, ...), custom_call_target="tpu_custom_call" | custom-call | tf_op jit(solution)/shard_map/pallas_call | solution.py:606
  38.9 1.6 %shard_map.96 = (bf16[64,1536]{1,0:T(8,128)(2,1)}, f32[7,2,15]{2,1,0:T(2,128)}) custom-call(bf16[64,1536]{1,0:T(8,128)(2,1)} %get-tuple-element.6.hidden_in, f32[7,2,15]{2,1,0:T(2,128)} %get-tuple-element.7.actions_in), custom_call_target="tpu_custom_call" | custom-call | tf_op jit(solution)/shard_map/pallas_call | solution.py:669

commit v9 on v8

--- a/solution.py
+++ b/solution.py
@@ -96,7 +96,7 @@
 
 
 HALVES = 2
-PIECES = 2
+PIECES = 4
 
 
 def nt_dot(lhs, rhs, **kw):

time: 40.6 us -> 40.7 us (level)
  no operation moved by 1% of the time
where the time goes in v9:
time: 40.7 us; the launch traced here: 40.5 us
  Pallas kernels  39.9 us (98%)
  between operations  0.64 us (2%)
    pallas_call x1, Pallas kernels, shards(): pl.pallas_call(functools.partial(fused_kernel, (S, H, U, heads, head_dim)...  38.3 us
    pallas_call x1, Pallas kernels, shards(): pl.pallas_call(write_kernel, out_shape=(jax.ShapeDtypeStruct(hidden.shape...  1.62 us

profile of v9, /device:TPU:0, one launch (start us, length us, event | category | flops | bytes accessed | tf_op | source)
XLA Modules:
  0.0 40.5 jit_solution(7006219071546278471)
XLA Ops:
  0.6 38.3 %shard_map.95 = (bf16[64,1536]{1,0:T(8,128)(2,1)}, f32[7,2,15]{2,1,0:T(2,128)}) custom-call(bf16[64,1536]{1,0:T(8,128)(2,1)} %frames.1, f32[1536]{0:T(1024)} %attn_gain_in.1, bf16[1152,1536]{1,0:T(8,128)(2,1)} %bitcast.5, bf16[384,1536]{1,0:T(8,128)(2,1)} %w_out.1, f32[1536]{0:T(1024)} %vit_gain_in.1, bf16[2,1536,256]{2,1,0:T(8,128)(2,1)} %w_pair.1, ...), custom_call_target="tpu_custom_call" | custom-call | tf_op jit(solution)/shard_map/pallas_call | solution.py:606
  38.9 1.6 %shard_map.96 = (bf16[64,1536]{1,0:T(8,128)(2,1)}, f32[7,2,15]{2,1,0:T(2,128)}) custom-call(bf16[64,1536]{1,0:T(8,128)(2,1)} %get-tuple-element.6.hidden_in, f32[7,2,15]{2,1,0:T(2,128)} %get-tuple-element.7.actions_in), custom_call_target="tpu_custom_call" | custom-call | tf_op jit(solution)/shard_map/pallas_call | solution.py:669
